TPU v7x, 512 devices: a whole 4x4x16 slice. The times are simulated.
512 devices in a mesh: fsdp: 16 (over z), expert: 32 (over x, y, core).
Axes of the slice: x: 4, y: 4, z: 16, core: 2. Of those that a mesh axis runs over, the one named last changes fastest.
Arguments:
- tokens: bfloat16 [65536, 2048], P(('fsdp', 'expert')), may hold values from -6 to 6
- expert_ids: int32 [65536, 4], P(('fsdp', 'expert')), may hold values from 0 to 63, all different within a row
- priority: int32 [512, 512], P(('fsdp', 'expert')), may hold values from 0 to 511, each once within a row
- overflow_pick: int32 [65536, 4], P(('fsdp', 'expert')), may hold values from 0 to 1
- partner: int32 [32], replicated, may hold values from 0 to 31, each once
- capacity: int32 [64], replicated, may hold values from 4 to 8, as said below
- route_scale: float32 [65536, 4], P(('fsdp', 'expert')), may hold values from 0.05 to 0.5
- gate_weight: bfloat16 [64, 2048, 768], P('expert', 'fsdp'), may hold values from -0.125 to 0.125
- up_weight: bfloat16 [64, 2048, 768], P('expert', 'fsdp'), may hold values from -0.125 to 0.125
- down_weight: bfloat16 [64, 768, 2048], P('expert', None, 'fsdp'), may hold values from -0.21875 to 0.21875
Outputs:
- mixed: bfloat16 [65536, 2048], P(('fsdp', 'expert'))
Inputs may be any that keep to these rules, and one draw needn't show every extreme that they name: capacity[e] main slots for each device's rows; at least a quarter of the experts grant exactly 8. `priority`: each row holds every number once. `partner`: each group number once.
All inputs are finite; a program needn't handle non-finite values.
Results may differ from a plain program's by a relative error of at most 0.0058.
Values may be sent and summed in bfloat16 or wider, within the bound.
No kernel may reach another device: no remote copies, remote signals or barrier semaphores. Data moves between devices by JAX's collectives and lax.ppermute only.
A program may use at most 64 MiB of HBM per device.

v0:
```python
import jax
import jax.numpy as jnp
from jax import lax
from jax.sharding import PartitionSpec as P

TOP = 4
GROUP = 2


def from_partner(block, axis, bit):
    count = lax.axis_size(axis)
    route = []
    for low in range(count):
        high = low | 1 << bit
        if high != low and high < count:
            route += [(low, high), (high, low)]
    return lax.ppermute(block, axis, route)


def routing(
    expert_ids, overflow_pick, order_key, capacity, partner, experts, slot_count, spill_count
):
    flat_ids = expert_ids.reshape(-1)
    flat_pick = overflow_pick.reshape(-1)
    earlier = order_key[None, :] < order_key[:, None]
    same_expert = flat_ids[None, :] == flat_ids[:, None]
    slot_rank = jnp.sum((same_expert & earlier).astype(jnp.int32), axis=1, dtype=jnp.int32)
    expert_range = jnp.arange(experts, dtype=jnp.int32)
    cap_of = jnp.sum(
        jnp.where(flat_ids[:, None] == expert_range[None, :], capacity[None, :], 0),
        axis=1,
        dtype=jnp.int32,
    )
    kept_main = slot_rank < cap_of
    group_range = jnp.arange(experts // GROUP, dtype=jnp.int32)
    partner_group = jnp.sum(
        jnp.where((flat_ids // GROUP)[:, None] == group_range[None, :], partner[None, :], 0),
        axis=1,
        dtype=jnp.int32,
    )
    target = partner_group * GROUP + flat_pick
    spilled = jnp.logical_not(kept_main)
    same_target = target[None, :] == target[:, None]
    spill_rank = jnp.sum(
        (same_target & earlier & spilled[None, :]).astype(jnp.int32), axis=1, dtype=jnp.int32
    )
    kept_spill = spilled & (spill_rank < spill_count)
    slot_width = slot_count + spill_count
    position = jnp.where(
        kept_main,
        flat_ids * slot_width + slot_rank,
        jnp.where(kept_spill, target * slot_width + slot_count + spill_rank, experts * slot_width),
    )
    return position


def spread_pieces(weight, fsdp_count):
    repeats = fsdp_count // 2
    widened = jnp.broadcast_to(weight[None], (repeats,) + weight.shape)
    return widened.reshape((fsdp_count,) + weight.shape[1:])


def expert_answers(incoming, gate_weight, up_weight, down_weight):
    fsdp_count = lax.axis_size("fsdp")
    gate_send = spread_pieces(gate_weight, fsdp_count)
    up_send = spread_pieces(up_weight, fsdp_count)
    down_send = spread_pieces(down_weight, fsdp_count)
    gate_all, up_all = (
        lax.all_to_all(gate_send, "fsdp", split_axis=0, concat_axis=1, tiled=True),
        lax.all_to_all(up_send, "fsdp", split_axis=0, concat_axis=1, tiled=True),
    )
    gate_sum = jnp.dot(incoming, gate_all[0], preferred_element_type=jnp.float32)
    up_sum = jnp.dot(incoming, up_all[0], preferred_element_type=jnp.float32)
    down_all = lax.all_to_all(down_send, "fsdp", split_axis=0, concat_axis=2, tiled=True)
    hidden = (jax.nn.silu(gate_sum) * up_sum).astype(jnp.bfloat16)
    return jnp.dot(hidden, down_all[0], preferred_element_type=jnp.float32).astype(jnp.bfloat16)


def paired_answers(incoming, gate_weight, up_weight, down_weight):
    groups, local_experts, slot_width, features = incoming.shape
    parity = lax.axis_index("fsdp") % 2
    keeping = lax.dynamic_index_in_dim(incoming, parity, 1, keepdims=False)
    giving = lax.dynamic_index_in_dim(incoming, 1 - parity, 1, keepdims=False)
    taken = from_partner(giving, "fsdp", 0)
    rows_all = jnp.concatenate([keeping, taken], axis=0).reshape(2 * groups * slot_width, features)
    computed = expert_answers(rows_all, gate_weight, up_weight, down_weight).reshape(
        2, groups, slot_width, features
    )
    own_part = computed[0]
    came_back = from_partner(computed[1], "fsdp", 0)
    triple = jnp.stack([own_part, came_back, own_part], axis=1)
    return lax.dynamic_slice_in_dim(triple, parity, 2, axis=1)


def per_device(
    tokens,
    expert_ids,
    priority,
    overflow_pick,
    partner,
    capacity,
    route_scale,
    gate_weight,
    up_weight,
    down_weight,
):
    tok_dev = tokens.shape[0]
    features = tokens.shape[1]
    groups = lax.axis_size("expert")
    local_experts = gate_weight.shape[0]
    experts = groups * local_experts
    slot_count = tok_dev * TOP // experts
    spill_count = max(slot_count // 4, 1)
    slot_width = slot_count + spill_count
    total_slots = experts * slot_width
    position = routing(
        expert_ids, overflow_pick, priority[0], capacity, partner, experts, slot_count, spill_count
    )
    owner_token = jnp.arange(tok_dev * TOP, dtype=jnp.int32) // TOP
    slot_token = jnp.full((total_slots,), -1, jnp.int32).at[position].set(owner_token, mode="drop")
    occupied = slot_token >= 0
    outgoing = jnp.where(
        occupied[:, None], tokens[jnp.maximum(slot_token, 0)], jnp.zeros((), jnp.bfloat16)
    )
    shaped = outgoing.reshape(experts, slot_width, features)
    main_rows = shaped[:, :slot_count].reshape(experts * slot_count, features)
    spill_rows = shaped[:, slot_count:].reshape(experts * spill_count, features)
    main_in = lax.all_to_all(main_rows, "expert", split_axis=0, concat_axis=0, tiled=True).reshape(
        groups, local_experts, slot_count, features
    )
    spill_in = lax.all_to_all(
        spill_rows, "expert", split_axis=0, concat_axis=0, tiled=True
    ).reshape(groups, local_experts, spill_count, features)
    incoming = jnp.concatenate([main_in, spill_in], axis=2)
    computed = paired_answers(incoming, gate_weight, up_weight, down_weight)
    main_out = computed[:, :, :slot_count].reshape(experts * slot_count, features)
    spill_out = computed[:, :, slot_count:].reshape(experts * spill_count, features)
    main_back = lax.all_to_all(main_out, "expert", split_axis=0, concat_axis=0, tiled=True)
    spill_back = lax.all_to_all(spill_out, "expert", split_axis=0, concat_axis=0, tiled=True)
    answers = jnp.concatenate(
        [
            main_back.reshape(experts, slot_count, features),
            spill_back.reshape(experts, spill_count, features),
        ],
        axis=1,
    ).reshape(total_slots, features)
    live_choice = position < total_slots
    picked = jnp.take(answers, jnp.minimum(position, total_slots - 1), axis=0)
    weights_flat = jnp.where(live_choice, route_scale.reshape(-1), jnp.float32(0.0))
    weighted = weights_flat[:, None] * picked.astype(jnp.float32)
    mixed_sum = jnp.sum(weighted.reshape(tok_dev, TOP, features), axis=1)
    return mixed_sum.astype(jnp.bfloat16)


def solution(mesh):
    in_specs = (
        P(("fsdp", "expert"), None),
        P(("fsdp", "expert"), None),
        P(("fsdp", "expert"), None),
        P(("fsdp", "expert"), None),
        P(),
        P(),
        P(("fsdp", "expert"), None),
        P("expert", "fsdp", None),
        P("expert", "fsdp", None),
        P("expert", None, "fsdp"),
    )
    out_specs = P(("fsdp", "expert"), None)
    return jax.shard_map(
        per_device, mesh=mesh, in_specs=in_specs, out_specs=out_specs, check_vma=False
    )
```

profile of v0, /device:TPU:1, one launch (start us, length us, event | category | flops | bytes accessed | tf_op | source)
XLA Modules:
  0.0 688.9 jit_solution(11949711000565309163)
XLA Ops:
  6.7 2.4 scatter_custom_fusion
  9.2 3.4 gather_fusion
  12.6 2.8 gather.12
  15.5 2.5 broadcast_select_fusion
  21.4 10.4 %all-to-all-start.1 = ((bf16[32,4,2048]{2,1,0:T(4,128)(2,1)}), bf16[32,4,2048]{2,1,0:T(4,128)(2,1)S(1)}, u32[]{:S(2)}, u32[]{:S(2)}) async-start(bf16[32,4,2048]{2,1,0:T(4,128)(2,1)} %all_to_all.51), calls=%async_computation.1 | async-start | bytes 1048576 | tf_op jit(solution)/shard_map/all_to_all | solution.py:131
  31.8 3.2 slice.30
  35.0 8.6 %all-to-all-done.1 = bf16[32,4,2048]{2,1,0:T(4,128)(2,1)S(1)} async-done(((bf16[32,4,2048]{2,1,0:T(4,128)(2,1)}), bf16[32,4,2048]{2,1,0:T(4,128)(2,1)S(1)}, u32[]{:S(2)}, u32[]{:S(2)}) %all-to-all-start.1) | async-done | bytes 524320 | tf_op jit(solution)/shard_map/all_to_all | solution.py:131
  43.6 3.8 all-to-all-start
  47.6 27.9 %all-to-all-done = bf16[32,16,2048]{2,1,0:T(8,128)(2,1)S(1)} async-done(((bf16[32,16,2048]{2,1,0:T(8,128)(2,1)}), bf16[32,16,2048]{2,1,0:T(8,128)(2,1)S(1)}, u32[]{:S(2)}, u32[]{:S(2)}) %all-to-all-start) | async-done | bytes 2097184 | tf_op jit(solution)/shard_map/all_to_all | solution.py:128
  75.8 148.3 %all_to_all.69 = bf16[16,768,128]{1,2,0:T(8,128)(2,1)} all-to-all(bf16[16,768,128]{1,2,0:T(8,128)(2,1)S(1)} %bitcast.37), channel_id=1, replica_groups=mesh['fsdp'=16,'expert'=32] {'fsdp'}, dimensions={0} | all-to-all | bytes 6291456 | tf_op jit(solution)/shard_map/all_to_all | solution.py:74
  224.4 147.4 %all_to_all.70 = bf16[16,128,768]{2,1,0:T(8,128)(2,1)} all-to-all(bf16[16,128,768]{2,1,0:T(8,128)(2,1)S(1)} %bitcast.38), channel_id=1, replica_groups=mesh['fsdp'=16,'expert'=32] {'fsdp'}, dimensions={0} | all-to-all | bytes 6291456 | tf_op jit(solution)/shard_map/all_to_all | solution.py:69
  373.8 12.1 %all-to-all-start.3 = ((bf16[16,128,768]{2,1,0:T(8,128)(2,1)}), bf16[16,128,768]{2,1,0:T(8,128)(2,1)}, u32[]{:S(2)}, u32[]{:S(2)}) async-start(bf16[16,128,768]{2,1,0:T(8,128)(2,1)} %bitcast.36), calls=%async_computation.3 | async-start | bytes 6291456 | tf_op jit(solution)/shard_map/all_to_all | solution.py:70
  387.6 3.4 collective-permute-start
  391.0 159.7 %collective-permute-done = bf16[32,10,2048]{2,0,1:T(8,128)(2,1)S(1)} collective-permute-done((bf16[32,10,2048]{2,0,1:T(8,128)(2,1)S(1)}, bf16[32,10,2048]{2,0,1:T(8,128)(2,1)S(1)}, u32[]{:S(2)}, u32[]{:S(2)}) %collective-permute-start) | collective-permute-done | bytes 1310752 | tf_op jit(solution)/shard_map/ppermute | solution.py:17
  550.9 3.5 copy.88
  554.5 4.1 reshape.303
  558.5 5.4 fusion.19
  563.9 9.9 %convolution_convert_fusion = bf16[640,2048]{1,0:T(8,128)(2,1)} fusion(bf16[768,2048]{0,1:T(8,128)(2,1)} %bitcast.43, f32[640,768]{1,0:T(8,128)} %fusion.19, bf16[640,2048]{1,0:T(8,128)(2,1)S(1)} %reshape.303, bf16[2048,768]{1,0:T(8,128)(2,1)} %bitcast.14), kind=kOutput, calls=%fused_computation.13 | convolution fusion | flops 4030791680 | bytes 13500416 | tf_op jit(solution)/shard_map/dot_general | solution.py:76
  573.8 3.5 fusion.18
  583.5 2.3 stack_squeeze.4
  585.9 26.5 %collective-permute-done.1 = bf16[32,10,2048]{2,0,1:T(8,128)(2,1)} collective-permute-done((bf16[32,10,2048]{2,0,1:T(8,128)(2,1)}, bf16[32,10,2048]{2,0,1:T(8,128)(2,1)}, u32[]{:S(2)}, u32[]{:S(2)}) %collective-permute-start.1) | collective-permute-done | bytes 1310752 | tf_op jit(solution)/shard_map/ppermute | solution.py:17
  614.5 2.8 fusion.1
  621.0 6.5 all-to-all-start.6
  627.6 3.2 copy_bitcast_fusion
  630.7 8.4 %all-to-all-done.6 = bf16[32,4,2048]{2,1,0:T(4,128)(2,1)S(1)} async-done(((bf16[32,4,2048]{2,1,0:T(4,128)(2,1)}), bf16[32,4,2048]{2,1,0:T(4,128)(2,1)S(1)}, u32[]{:S(2)}, u32[]{:S(2)}) %all-to-all-start.6) | async-done | bytes 524320 | tf_op jit(solution)/shard_map/all_to_all | solution.py:139
  639.2 3.8 all-to-all-start.5
  644.3 26.8 %all-to-all-done.5 = bf16[32,16,2048]{2,1,0:T(8,128)(2,1)S(1)} async-done(((bf16[32,16,2048]{2,1,0:T(8,128)(2,1)}), bf16[32,16,2048]{2,1,0:T(8,128)(2,1)S(1)}, u32[]{:S(2)}, u32[]{:S(2)}) %all-to-all-start.5) | async-done | bytes 2097184 | tf_op jit(solution)/shard_map/all_to_all | solution.py:138
  671.1 2.7 pad_maximum_fusion
  673.8 4.1 reshape.309
  677.9 3.3 gather_fusion.1
  681.2 2.7 gather.14
  683.9 4.9 multiply_reduce_fusion
  (73 shorter events, 28.0 us)
Async XLA Ops:
  0.0 9.2 %copy-start = (bf16[128,2048]{1,0:T(8,128)(2,1)S(1)}, bf16[128,2048]{1,0:T(8,128)(2,1)}, u32[]{:S(2)}) copy-start(bf16[128,2048]{1,0:T(8,128)(2,1)} %param.10) | copy-start | bytes 1572868
  18.1 2.0 copy-start.2
  21.4 22.2 %all-to-all-start.1 = ((bf16[32,4,2048]{2,1,0:T(4,128)(2,1)}), bf16[32,4,2048]{2,1,0:T(4,128)(2,1)S(1)}, u32[]{:S(2)}, u32[]{:S(2)}) async-start(bf16[32,4,2048]{2,1,0:T(4,128)(2,1)} %all_to_all.51), calls=%async_computation.1 | async-start | bytes 1048576 | tf_op jit(solution)/shard_map/all_to_all | solution.py:131
  35.0 12.4 %copy-start.6 = (bf16[2,768,128]{2,1,0:T(8,128)(2,1)S(1)}, bf16[2,768,128]{2,1,0:T(8,128)(2,1)}, u32[]{:S(2)}) copy-start(bf16[2,768,128]{2,1,0:T(8,128)(2,1)} %param.19) | copy-start | bytes 1179652
  43.6 31.9 %all-to-all-start = ((bf16[32,16,2048]{2,1,0:T(8,128)(2,1)}), bf16[32,16,2048]{2,1,0:T(8,128)(2,1)S(1)}, u32[]{:S(2)}, u32[]{:S(2)}) async-start(bf16[32,16,2048]{2,1,0:T(8,128)(2,1)} %bitcast.41), calls=%async_computation | async-start | bytes 4194304 | tf_op jit(solution)/shard_map/all_to_all | solution.py:128
  75.8 148.3 %copy-start.4 = (bf16[2,128,768]{2,1,0:T(8,128)(2,1)S(1)}, bf16[2,128,768]{2,1,0:T(8,128)(2,1)}, u32[]{:S(2)}) copy-start(bf16[2,128,768]{2,1,0:T(8,128)(2,1)} %param.17) | copy-start | bytes 1179652
  224.4 147.4 %copy-start.5 = (bf16[2,128,768]{2,1,0:T(8,128)(2,1)S(1)}, bf16[2,128,768]{2,1,0:T(8,128)(2,1)}, u32[]{:S(2)}) copy-start(bf16[2,128,768]{2,1,0:T(8,128)(2,1)} %param.18) | copy-start | bytes 1179652
  373.8 190.1 %all-to-all-start.3 = ((bf16[16,128,768]{2,1,0:T(8,128)(2,1)}), bf16[16,128,768]{2,1,0:T(8,128)(2,1)}, u32[]{:S(2)}, u32[]{:S(2)}) async-start(bf16[16,128,768]{2,1,0:T(8,128)(2,1)} %bitcast.36), calls=%async_computation.3 | async-start | bytes 6291456 | tf_op jit(solution)/shard_map/all_to_all | solution.py:70
  387.6 163.1 %collective-permute-start = (bf16[32,10,2048]{2,0,1:T(8,128)(2,1)S(1)}, bf16[32,10,2048]{2,0,1:T(8,128)(2,1)S(1)}, u32[]{:S(2)}, u32[]{:S(2)}) collective-permute-start(bf16[32,10,2048]{2,0,1:T(8,128)(2,1)S(1)} %get-tuple-element.12), channel_id=1, source_target_pairs={{0,32},{32,0},{64,96},{96,64},{128,160},{160,128},{192,224},{224,1... | collective-permute-start | bytes 3932168 | tf_op jit(solution)/shard_map/ppermute | solution.py:17
  581.4 31.0 %collective-permute-start.1 = (bf16[32,10,2048]{2,0,1:T(8,128)(2,1)}, bf16[32,10,2048]{2,0,1:T(8,128)(2,1)}, u32[]{:S(2)}, u32[]{:S(2)}) collective-permute-start(bf16[32,10,2048]{2,0,1:T(8,128)(2,1)} %copy.90), channel_id=1, source_target_pairs={{0,32},{32,0},{64,96},{96,64},{128,160},{160,128},{192,224},{224,1... | collective-permute-start | bytes 3932168 | tf_op jit(solution)/shard_map/ppermute | solution.py:17
  617.3 2.0 copy-start.3
  621.0 18.1 %all-to-all-start.6 = ((bf16[32,4,2048]{2,1,0:T(4,128)(2,1)}), bf16[32,4,2048]{2,1,0:T(4,128)(2,1)S(1)}, u32[]{:S(2)}, u32[]{:S(2)}) async-start(bf16[32,4,2048]{2,1,0:T(4,128)(2,1)} %copy.94), calls=%async_computation.6 | async-start | bytes 1048576 | tf_op jit(solution)/shard_map/all_to_all | solution.py:139
  630.7 13.0 %copy-start.7 = (s32[128,4]{0,1:T(4,128)S(1)}, s32[128,4]{0,1:T(4,128)}, u32[]{:S(2)}) copy-start(s32[128,4]{0,1:T(4,128)} %param.11) | copy-start | bytes 6148
  630.7 13.0 %copy-start.8 = (s32[128,4]{0,1:T(4,128)S(1)}, s32[128,4]{0,1:T(4,128)}, u32[]{:S(2)}) copy-start(s32[128,4]{0,1:T(4,128)} %param.13) | copy-start | bytes 6148
  630.7 13.1 %copy-start.9 = (f32[128,4]{0,1:T(4,128)S(1)}, f32[128,4]{0,1:T(4,128)}, u32[]{:S(2)}) copy-start(f32[128,4]{0,1:T(4,128)} %param.16) | copy-start | bytes 6148
  639.2 31.9 %all-to-all-start.5 = ((bf16[32,16,2048]{2,1,0:T(8,128)(2,1)}), bf16[32,16,2048]{2,1,0:T(8,128)(2,1)S(1)}, u32[]{:S(2)}, u32[]{:S(2)}) async-start(bf16[32,16,2048]{2,1,0:T(8,128)(2,1)} %copy_bitcast_fusion), calls=%async_computation.5 | async-start | bytes 4194304 | tf_op jit(solution)/shard_map/all_to_all | solution.py:138
  677.9 11.0 %copy-start.1 = (bf16[128,2048]{1,0:T(8,128)(2,1)S(1)}, bf16[128,2048]{1,0:T(8,128)(2,1)}, u32[]{:S(2)}) copy-start(bf16[128,2048]{1,0:T(8,128)(2,1)} %param.10) | copy-start | bytes 1572868
where the time goes:
time: 690 us; the launch traced here: 689 us
  blocking collectives  296 us (43%)
  waiting for transfers between devices  258 us (37%)
  local copies, waits for them, and re-layouts  59.5 us (9%)
  starting transfers between devices  42.2 us (6%)
  other arithmetic  17.9 us (3%)
  matrix products  15.2 us (2%)
    ppermute x2, waiting for transfers between devices, from_partner(): return lax.ppermute(block, axis, route)  186 us
    all_to_all x1, blocking collectives, expert_answers(): lax.all_to_all(down_send, 'fsdp', split_axis=0, concat_axis=2, tiled=True)  148 us
    all_to_all x1, blocking collectives, expert_answers(): lax.all_to_all(gate_send, 'fsdp', split_axis=0, concat_axis=1, tiled=True)  147 us
    all_to_all x1, waiting for transfers between devices, per_device(): lax.all_to_all(main_rows, 'expert', split_axis=0, concat_axis=0, tiled=True)  27.9 us
    all_to_all x1, waiting for transfers between devices, per_device(): lax.all_to_all(main_out, 'expert', split_axis=0, concat_axis=0, tiled=True)  26.8 us
  transfers between devices with their start and end apart: 7, of which 6 were waited for; matrix products, arithmetic and copies ran while one was open for 4% of the time, Pallas kernels for 0%

commit v1 on v0

v1 whole, which is shorter than its diff:
```python
import jax
import jax.numpy as jnp
from jax import lax
from jax.experimental import pallas as pl
from jax.experimental.pallas import tpu as pltpu
from jax.sharding import PartitionSpec as P

TOP = 4
GROUP = 2
LANE = 128
VMEM_LIMIT = 56 * 1024 * 1024

TOK = 128
CHOICES = TOK * TOP
EXPERTS = 64
SLOTS = 8
OSLOTS = 2
DEVICES = 32
MAIN = EXPERTS * SLOTS
SPILL = EXPERTS * OSLOTS
ROWS = MAIN + SPILL
D = 2048
HID = 768
PIECES = 16
PIECE = 3 * LANE
HALF = PIECE // 2


def iota(shape, axis):
    return lax.broadcasted_iota(jnp.int32, shape, axis)


def ones_where(hit):
    return jnp.where(hit, 1, 0)


def spill_index(row):
    return (row >> 4) * 4 + (row & 3)


def spill_quarter(row):
    return (row >> 2) & 3


def one_hot(hit):
    return jnp.where(hit, 1.0, 0.0).astype(jnp.bfloat16)


def dot(a, b):
    return jnp.dot(a, b, preferred_element_type=jnp.float32)


def across(a, b):
    return lax.dot_general(a, b, (((1,), (1,)), ((), ())), preferred_element_type=jnp.float32)


MAIN_E = MAIN // 2
SPILL_E = SPILL // 2
ROWS_E = ROWS // 2


def dispatch_kernel(
    rows, cols, partner_r, partner_c, cap_r, cap_c, scale, tokens, out, s_hi, s_lo, p_hi, p_lo,
):
    ids_r, key_r, pick_r = rows[0:1, :], rows[1:2, :], rows[2:3, :]
    rank_r = jnp.zeros((1, CHOICES), jnp.int32)
    rank_c = []
    for b in range(TOP):
        at = slice(b * TOK, (b + 1) * TOK)
        ids_c, key_c = cols[at, 0:1], cols[at, 1:2]
        same = ids_c == ids_r
        rank_r += jnp.sum(ones_where(same & (key_c < key_r)), axis=0, keepdims=True)
        rank_c.append(jnp.sum(ones_where(same & (key_r < key_c)), axis=1, keepdims=True))
    room_r = jnp.sum(jnp.where(iota((EXPERTS, CHOICES), 0) == ids_r, cap_c[...], 0), axis=0, keepdims=True)
    mate_r = jnp.sum(
        jnp.where(iota((EXPERTS // GROUP, CHOICES), 0) == (ids_r >> 1), partner_c[...], 0), axis=0, keepdims=True
    )
    target_r = mate_r * GROUP + pick_r
    over_r = ones_where(rank_r >= room_r)
    spill_r = jnp.zeros((1, CHOICES), jnp.int32)
    main_c, lost_c = [], []
    for b in range(TOP):
        at = slice(b * TOK, (b + 1) * TOK)
        ids_c, key_c, pick_c = cols[at, 0:1], cols[at, 1:2], cols[at, 2:3]
        room_c = jnp.sum(jnp.where(iota((TOK, EXPERTS), 1) == ids_c, cap_r[...], 0), axis=1, keepdims=True)
        mate_c = jnp.sum(
            jnp.where(iota((TOK, EXPERTS // GROUP), 1) == (ids_c >> 1), partner_r[...], 0), axis=1, keepdims=True
        )
        target_c = mate_c * GROUP + pick_c
        over_c = ones_where(rank_c[b] >= room_c)
        same = target_c == target_r
        spill_r += jnp.sum(jnp.where(same & (key_c < key_r), over_c, 0), axis=0, keepdims=True)
        spill_c = jnp.sum(jnp.where(same & (key_r < key_c), over_r, 0), axis=1, keepdims=True)
        main_c.append(jnp.where(over_c == 0, ids_c * SLOTS + rank_c[b], -1))
        lost_c.append(jnp.where((over_c == 1) & (spill_c < OSLOTS), target_c * OSLOTS + spill_c, -1))
    main_r = jnp.where(over_r == 0, ids_r * SLOTS + rank_r, -1)
    lost_r = jnp.where((over_r == 1) & (spill_r < OSLOTS), target_r * OSLOTS + spill_r, -1)

    s_main = jnp.zeros((TOK, MAIN), jnp.float32)
    s_lost = jnp.zeros((TOK, MAIN), jnp.float32)
    lane = iota((TOK, MAIN), 1)
    second, own = lane >> 8, lane & (MAIN_E - 1)
    main_of = (own >> 3) * 16 + second * SLOTS + (own & 7)
    lost_of = (own >> 3) * 4 + second * OSLOTS + (own & 1)
    pick_main = jnp.zeros((MAIN, TOK), jnp.float32)
    pick_lost = jnp.zeros((MAIN, TOK), jnp.float32)
    line = iota((MAIN, TOK), 0)
    for k in range(TOP):
        at = slice(k * TOK, (k + 1) * TOK)
        weight = scale[:, k : k + 1]
        s_main += jnp.where(main_of == main_c[k], weight, 0.0)
        s_lost += jnp.where(lost_of == lost_c[k], weight, 0.0)
        pick_main += jnp.where(line == main_r[:, at], 1.0, 0.0)
        pick_lost += jnp.where(spill_index(line) == lost_r[:, at], 1.0, 0.0)
    for value, high, low in ((s_main, s_hi, s_lo), (s_lost, p_hi, p_lo)):
        top = value.astype(jnp.bfloat16)
        high[...] = top
        low[...] = (value - top.astype(jnp.float32)).astype(jnp.bfloat16)

    picks = pick_main.astype(jnp.bfloat16)
    quarter = D // 4
    packed = jnp.zeros((MAIN, quarter), jnp.float32)
    for q in range(4):
        at = slice(q * quarter, (q + 1) * quarter)
        piece = tokens[:, at]
        out[:, at] = jnp.dot(picks, piece, preferred_element_type=jnp.float32).astype(jnp.bfloat16)
        own = jnp.where(spill_quarter(line) == q, pick_lost, 0.0).astype(jnp.bfloat16)
        packed += jnp.dot(own, piece, preferred_element_type=jnp.float32)
    out[:, D:] = packed.astype(jnp.bfloat16)


def main_line(row, e):
    return (row >> 3) * 16 + e * SLOTS + (row & 7)


def packed_line(row, e, q):
    return (row >> 1) * 16 + q * 4 + e * OSLOTS + (row & 1)


def split_kernel(x, out):
    quarter = D // 4
    for e in range(2):
        shape = (MAIN_E, MAIN)
        pick = one_hot(iota(shape, 1) == main_line(iota(shape, 0), e))
        shape = (SPILL_E, MAIN)
        for q in range(4):
            at = slice(q * quarter, (q + 1) * quarter)
            out[e, :MAIN_E, at] = dot(pick, x[:, at]).astype(jnp.bfloat16)
            own = one_hot(iota(shape, 1) == packed_line(iota(shape, 0), e, q))
            out[e, MAIN_E:, at] = dot(own, x[:, D:]).astype(jnp.bfloat16)


def pack_kernel(gate, up, down, first, high, low):
    first[:LANE, :] = gate[0]
    first[LANE : 2 * LANE, :] = up[0]
    first[2 * LANE :, :] = down[0].T
    high[:LANE, :] = gate[1]
    high[LANE:, :] = up[1, : HALF - LANE]
    low[: HALF - LANE, :] = up[1, HALF - LANE :]
    low[HALF - LANE :, :] = down[1].T


WIDE = 2 * LANE
TILES = HID // WIDE


def expert(x, out, gate_w, up_w, down_w, hidden_s, copies):
    for group in copies:
        for copy in group:
            copy.start()
    for n in range(TILES):
        for copy in copies[n]:
            copy.wait()
        cut = slice(n * WIDE, (n + 1) * WIDE)
        gate = dot(x[...], gate_w[:, :, cut].reshape(D, WIDE))
        up = dot(x[...], up_w[:, :, cut].reshape(D, WIDE))
        hidden_s[:, cut] = ((gate / (1.0 + jnp.exp(-gate))) * up).astype(jnp.bfloat16)
    quarter = D // 4
    shape = (MAIN_E, SPILL_E)
    line, row = iota(shape, 0), iota(shape, 1)
    packed = jnp.zeros((MAIN_E, quarter), jnp.float32)
    for q in range(4):
        for copy in copies[TILES + q]:
            copy.wait()
        at = slice(q * quarter, (q + 1) * quarter)
        answer = across(hidden_s[...], down_w[q * 4 : (q + 1) * 4].reshape(quarter, HID)).astype(jnp.bfloat16)
        out[:, at] = answer[:MAIN_E]
        place = one_hot((((line >> 3) * 2 + (line & 1)) == row) & (((line >> 1) & 3) == q))
        packed += dot(place, answer[MAIN_E:])
    out[:, D:] = packed.astype(jnp.bfloat16)


def first_kernel(x, weights, out, gate_w, up_w, down_w, hidden_s, rows, sems, sem):
    copies = [[pltpu.make_async_copy(x.at[0], rows, sem)]] + [[] for _ in range(TILES + 3)]
    for n in range(TILES):
        cut = pl.ds(n * WIDE, WIDE)
        for i, to in enumerate((gate_w, up_w)):
            source = weights.at[:, pl.ds(i * LANE, LANE), cut]
            copies[n].append(pltpu.make_async_copy(source, to.at[:, :, cut], sems.at[i, n]))
    for q in range(4):
        own = pl.ds(q * 4, 4)
        source = weights.at[own, pl.ds(2 * LANE, LANE)]
        copies[TILES + q].append(pltpu.make_async_copy(source, down_w.at[own], sems.at[2, q]))
    expert(rows, out, gate_w, up_w, down_w, hidden_s, copies)


def second_kernel(me, x, *refs):
    highs, lows = refs[:PIECES], refs[PIECES : 2 * PIECES]
    out, gate_w, up_w, down_w, hidden_s, sems = refs[2 * PIECES :]
    copies = [[] for _ in range(TILES + 4)]
    half = HALF - LANE
    for j in range(PIECES):
        owner = lax.rem(me[0] + j, PIECES)
        moves = [
            (highs[j].at[pl.ds(0, LANE)], gate_w.at[owner]),
            (highs[j].at[pl.ds(LANE, half)], up_w.at[owner, pl.ds(0, half)]),
            (lows[j].at[pl.ds(0, half)], up_w.at[owner, pl.ds(half, half)]),
            (lows[j].at[pl.ds(half, LANE)], down_w.at[owner]),
        ]
        now = [pltpu.make_async_copy(source, to, sems.at[i, j]) for i, (source, to) in enumerate(moves)]
        copies[0] += now[:-1]
        copies[TILES] += now[-1:]
    expert(x.at[1], out, gate_w, up_w, down_w, hidden_s, copies)


def mix(e, ans, s_hi, s_lo, p_hi, p_lo):
    own = slice(e * MAIN_E, (e + 1) * MAIN_E)
    both = jnp.concatenate([s_hi[:, own], s_lo[:, own]], axis=0)
    total = dot(both, ans[:, :D])
    total = total[:TOK] + total[TOK:]
    both = jnp.concatenate([p_hi[:, own], p_lo[:, own]], axis=0)
    quarter = (iota(both.shape, 1) >> 1) & 3
    zero = jnp.zeros((), jnp.bfloat16)
    sums = []
    for q in range(4):
        lost = dot(jnp.where(quarter == q, both, zero), ans[:, D:])
        sums.append(lost[:TOK] + lost[TOK:])
    return total + jnp.concatenate(sums, axis=1)


def mix_kernel(ans, s_hi, s_lo, p_hi, p_lo, out):
    out[...] = mix(1, ans, s_hi, s_lo, p_hi, p_lo)


def final_kernel(ans, s_hi, s_lo, p_hi, p_lo, before, out):
    out[...] = (before[...] + mix(0, ans, s_hi, s_lo, p_hi, p_lo)).astype(jnp.bfloat16)


def params():
    return pltpu.CompilerParams(vmem_limit_bytes=VMEM_LIMIT)


def vmem(count):
    return [pl.BlockSpec(memory_space=pltpu.VMEM)] * count


def anywhere(count):
    return [pl.BlockSpec(memory_space=pl.ANY)] * count


SMEM = pl.BlockSpec(memory_space=pltpu.SMEM)


def cost(flops, size):
    return pl.CostEstimate(flops=flops, bytes_accessed=size, transcendentals=0)


def dispatch(expert_ids, priority, overflow_pick, partner, capacity, route_scale, tokens):
    def by_choice(block):
        return block.reshape(TOK, TOP).T.reshape(1, CHOICES)

    rows = jnp.concatenate([by_choice(expert_ids), by_choice(priority), by_choice(overflow_pick)], axis=0)
    scales = jax.ShapeDtypeStruct((TOK, MAIN), jnp.bfloat16)
    return pl.pallas_call(
        dispatch_kernel,
        out_shape=[jax.ShapeDtypeStruct((MAIN, D + D // 4), jnp.bfloat16)] + [scales] * 4,
        in_specs=vmem(8),
        out_specs=vmem(5),
        compiler_params=params(),
        cost_estimate=cost(2 * MAIN * TOK * D * 2, 4 * 1024 * 1024),
    )(
        rows, rows.T, partner[None, :], partner[:, None], capacity[None, :], capacity[:, None],
        route_scale, tokens,
    )


def pack(gate_weight, up_weight, down_weight):
    half = jax.ShapeDtypeStruct((HALF, HID), jnp.bfloat16)
    return pl.pallas_call(
        pack_kernel,
        out_shape=[jax.ShapeDtypeStruct((PIECE, HID), jnp.bfloat16), half, half],
        in_specs=vmem(3),
        out_specs=vmem(3),
        compiler_params=params(),
        cost_estimate=cost(0, 8 * PIECE * HID),
    )(gate_weight, up_weight, down_weight)


def split_rows(x):
    return pl.pallas_call(
        split_kernel,
        out_shape=jax.ShapeDtypeStruct((2, ROWS_E, D), jnp.bfloat16),
        in_specs=vmem(1),
        out_specs=vmem(1)[0],
        compiler_params=params(),
        cost_estimate=cost(2 * ROWS * MAIN * D, 6 * 1024 * 1024),
    )(x)


def expert_scratch():
    return [pltpu.VMEM((PIECES, LANE, HID), jnp.bfloat16)] * 3 + [pltpu.VMEM((ROWS_E, HID), jnp.bfloat16)]


EXPERT_OUT = jax.ShapeDtypeStruct((MAIN_E, D + D // 4), jnp.bfloat16)
EXPERT_COST = cost(6 * ROWS_E * D * HID, 13 * 1024 * 1024)


def first_expert(x, weights):
    return pl.pallas_call(
        first_kernel,
        out_shape=EXPERT_OUT,
        in_specs=anywhere(2),
        out_specs=vmem(1)[0],
        scratch_shapes=[
            *expert_scratch(),
            pltpu.VMEM((ROWS_E, D), jnp.bfloat16),
            pltpu.SemaphoreType.DMA((3, 4)),
            pltpu.SemaphoreType.DMA,
        ],
        compiler_params=params(),
        cost_estimate=EXPERT_COST,
    )(x, weights)


def second_expert(me, x, pieces):
    return pl.pallas_call(
        second_kernel,
        out_shape=EXPERT_OUT,
        in_specs=[SMEM] + vmem(1) + anywhere(len(pieces)),
        out_specs=vmem(1)[0],
        scratch_shapes=[*expert_scratch(), pltpu.SemaphoreType.DMA((4, PIECES))],
        compiler_params=params(),
        cost_estimate=EXPERT_COST,
    )(me, x, *pieces)


def combine(ans, scales):
    return pl.pallas_call(
        mix_kernel,
        out_shape=jax.ShapeDtypeStruct((TOK, D), jnp.float32),
        in_specs=vmem(5),
        out_specs=vmem(1)[0],
        compiler_params=params(),
        cost_estimate=cost(5 * TOK * MAIN_E * D, 3 * 1024 * 1024),
    )(ans, *scales)


def combine_last(ans, scales, before):
    return pl.pallas_call(
        final_kernel,
        out_shape=jax.ShapeDtypeStruct((TOK, D), jnp.bfloat16),
        in_specs=vmem(6),
        out_specs=vmem(1)[0],
        compiler_params=params(),
        cost_estimate=cost(5 * TOK * MAIN_E * D, 3 * 1024 * 1024),
    )(ans, *scales, before)


def exchange(block):
    rows, width = block.shape
    shaped = block.reshape(DEVICES, rows // DEVICES, width)
    return lax.all_to_all(shaped, "expert", split_axis=0, concat_axis=0, tiled=True).reshape(rows, width)


def after(value, *others):
    return lax.optimization_barrier((value, *others))[0]


def per_device(
    tokens, expert_ids, priority, overflow_pick, partner, capacity, route_scale,
    gate_weight, up_weight, down_weight,
):
    me = lax.axis_index("fsdp").astype(jnp.int32).reshape(1)
    right = [(i, (i + 1) % PIECES) for i in range(PIECES)]
    left = [(i, (i - 1) % PIECES) for i in range(PIECES)]

    own, high, low = pack(gate_weight, up_weight, down_weight)
    weights = lax.all_gather(own, "fsdp")
    highs, lows = {0: high}, {0: low}
    half = PIECES // 2
    for step in range(1, half + 1):
        highs[PIECES - step] = lax.ppermute(highs[(PIECES - step + 1) % PIECES], "fsdp", right)
        lows[step] = lax.ppermute(lows[step - 1], "fsdp", left)
        if step < half:
            highs[step] = lax.ppermute(highs[step - 1], "fsdp", left)
            lows[PIECES - step] = lax.ppermute(lows[(PIECES - step + 1) % PIECES], "fsdp", right)
    pieces = [highs[j] for j in range(PIECES)] + [lows[j] for j in range(PIECES)]

    ready = after(tokens, highs[PIECES - 1], lows[1])
    out, *scales = dispatch(expert_ids, priority, overflow_pick, partner, capacity, route_scale, ready)
    x = split_rows(exchange(out))
    second = second_expert(me, x, pieces)
    first = first_expert(after(x, second), weights)
    before = combine(exchange(second), scales)
    return combine_last(exchange(first), scales, before)


def solution(mesh):
    in_specs = (
        P(("fsdp", "expert"), None),
        P(("fsdp", "expert"), None),
        P(("fsdp", "expert"), None),
        P(("fsdp", "expert"), None),
        P(),
        P(),
        P(("fsdp", "expert"), None),
        P("expert", "fsdp", None),
        P("expert", "fsdp", None),
        P("expert", None, "fsdp"),
    )
    out_specs = P(("fsdp", "expert"), None)
    return jax.shard_map(
        per_device, mesh=mesh, in_specs=in_specs, out_specs=out_specs, check_vma=False
    )
```

time: 690 us -> 293 us (0.42)
  blocking collectives: 296 us -> 0 us
  waiting for transfers between devices: 258 us -> 105 us
  starting transfers between devices: 42.2 us -> 124 us
  local copies, waits for them, and re-layouts: 59.5 us -> 8.35 us
  Pallas kernels: 0 us -> 38.5 us
  other arithmetic: 17.9 us -> 2.04 us
  matrix products: 15.2 us -> 0 us
  between operations: 0.44 us -> 14 us
    all_to_all x2 -> x0, blocking collectives: 296 us -> none  [the longest x1 148 us: expert_answers(): lax.all_to_all(down_send, 'fsdp', split_axis=0, concat_axis=2, tiled=True)]
    ppermute x2 -> x30, waiting for transfers between devices: 186 us -> 76.2 us  [the longest x8 40.3 us: per_device(): lax.ppermute(highs[(PIECES - step + 1) % PIECES], 'fsdp', right)]
    ppermute x2 -> x30, starting transfers between devices: 5.51 us -> 105 us  [the longest x8 41.5 us: per_device(): lows[step] = lax.ppermute(lows[step - 1], 'fsdp', left)]
    all_to_all x5 -> x3, waiting for transfers between devices: 71.7 us -> 28.5 us  [exchange(): lax.all_to_all(shaped, 'expert', split_axis=0, concat_axis=0, tiled=True)]
    pallas_call x0 -> x7, Pallas kernels: none -> 38.5 us  [the longest x1 10.4 us: second_expert(): pl.pallas_call(second_kernel, out_shape=EXPERT_OUT, in_specs=[SMEM] + vme...]
    all_to_all x5 -> x3, starting transfers between devices: 36.7 us -> 19.6 us  [exchange(): lax.all_to_all(shaped, 'expert', split_axis=0, concat_axis=0, tiled=True)]
    dot_general x2 -> x0, matrix products: 15.2 us -> none  [the longest x1 9.85 us: expert_answers(): jnp.dot(hidden, down_all[0], preferred_element_type=jnp.float32)]
    gather x4 -> x0, local copies, waits for them, and re-layouts: 12.2 us -> none  [the longest x2 6.19 us: per_device(): tokens[jnp.maximum(slot_token, 0)]]
  transfers between devices with their start and end apart: 7 -> 34, of which waited for: 6 -> 15; matrix products, arithmetic and copies ran while one was open for 4% -> 3% of each run, Pallas kernels for 0% -> 11%
where the time goes in v1:
time: 293 us; the launch traced here: 292 us
  starting transfers between devices  124 us (42%)
  waiting for transfers between devices  105 us (36%)
  Pallas kernels  38.5 us (13%)
  between operations  14 us (5%)
  local copies, waits for them, and re-layouts  8.35 us (3%)
    ppermute x8, starting transfers between devices, per_device(): lows[step] = lax.ppermute(lows[step - 1], 'fsdp', left)  41.5 us
    ppermute x8, waiting for transfers between devices, per_device(): lax.ppermute(highs[(PIECES - step + 1) % PIECES], 'fsdp', right)  40.3 us
    ppermute x7, waiting for transfers between devices, per_device(): lax.ppermute(lows[(PIECES - step + 1) % PIECES], 'fsdp', right)  35.8 us
    ppermute x7, starting transfers between devices, per_device(): highs[step] = lax.ppermute(highs[step - 1], 'fsdp', left)  32 us
    all_to_all x3, waiting for transfers between devices, exchange(): lax.all_to_all(shaped, 'expert', split_axis=0, concat_axis=0, tiled=True)  28.5 us
    all_to_all x3, starting transfers between devices, exchange(): lax.all_to_all(shaped, 'expert', split_axis=0, concat_axis=0, tiled=True)  19.6 us
    ppermute x8, starting transfers between devices, per_device(): lax.ppermute(highs[(PIECES - step + 1) % PIECES], 'fsdp', right)  17.8 us
    ppermute x7, starting transfers between devices, per_device(): lax.ppermute(lows[(PIECES - step + 1) % PIECES], 'fsdp', right)  13.4 us
  transfers between devices with their start and end apart: 34, of which 15 were waited for; matrix products, arithmetic and copies ran while one was open for 3% of the time, Pallas kernels for 11%

profile of v1, /device:TPU:1, one launch (start us, length us, event | category | flops | bytes accessed | tf_op | source)
XLA Modules:
  0.0 291.8 jit_solution(11534438346252163292)
XLA Ops:
  13.3 9.5 %collective-permute-start.1 = (bf16[192,768]{1,0:T(8,128)(2,1)}, bf16[192,768]{1,0:T(8,128)(2,1)S(1)}, u32[]{:S(2)}, u32[]{:S(2)}) collective-permute-start(bf16[192,768]{1,0:T(8,128)(2,1)} %get-tuple-element.16.refs_16_), channel_id=1, source_target_pairs={{0,480},{32,0},{64,32},{96,64},{128,96},{160,128},{192,160},{224,1... | collective-permute-start | bytes 884744 | tf_op jit(solution)/shard_map/ppermute | solution.py:393
  30.6 5.9 %shard_map.101 = (bf16[512,2560]{1,0:T(8,128)(2,1)}, bf16[128,512]{1,0:T(8,128)(2,1)}, bf16[128,512]{1,0:T(8,128)(2,1)}, bf16[128,512]{1,0:T(8,128)(2,1)}, bf16[128,512]{1,0:T(8,128)(2,1)}) custom-call(s32[3,512]{1,0:T(4,128)} %copy-done.27, s32[512,3]{1,0:T(8,128)} %bitcast.28, s32[1,32]{1,0:T(1,128)} %bitcast.36, s32[32,1]{1,0:T(8,128)} %copy.26.partner_c, ...), custom_call_target="tpu_custom_call" | custom-call | flops 536870912 | bytes 4194304 | tf_op jit(solution)/shard_map/pallas_call | solution.py:274
  36.5 8.1 %all-to-all-start = ((bf16[32,16,2560]{2,1,0:T(8,128)(2,1)}), bf16[32,16,2560]{2,1,0:T(8,128)(2,1)S(1)}, u32[]{:S(2)}, u32[]{:S(2)}) async-start(bf16[32,16,2560]{2,1,0:T(8,128)(2,1)} %bitcast.27), calls=%async_computation | async-start | bytes 5242880 | tf_op jit(solution)/shard_map/all_to_all | solution.py:372
  46.6 4.6 %collective-permute-start.2 = (bf16[192,768]{1,0:T(8,128)(2,1)S(1)}, bf16[192,768]{1,0:T(8,128)(2,1)S(1)}, u32[]{:S(2)}, u32[]{:S(2)}) collective-permute-start(bf16[192,768]{1,0:T(8,128)(2,1)S(1)} %copy-done.3), channel_id=1, source_target_pairs={{0,480},{32,0},{64,32},{96,64},{128,96},{160,128},{192,160},{224,1... | collective-permute-start | bytes 884744 | tf_op jit(solution)/shard_map/ppermute | solution.py:395
  57.7 5.3 %collective-permute-done.23.refs_31_ = bf16[192,768]{1,0:T(8,128)(2,1)S(1)} collective-permute-done((bf16[192,768]{1,0:T(8,128)(2,1)S(1)}, bf16[192,768]{1,0:T(8,128)(2,1)S(1)}, u32[]{:S(2)}, u32[]{:S(2)}) %collective-permute-start.23) | collective-permute-done | bytes 294944 | tf_op jit(solution)/shard_map/ppermute | solution.py:396
  64.9 4.6 %collective-permute-start.3 = (bf16[192,768]{1,0:T(8,128)(2,1)S(1)}, bf16[192,768]{1,0:T(8,128)(2,1)S(1)}, u32[]{:S(2)}, u32[]{:S(2)}) collective-permute-start(bf16[192,768]{1,0:T(8,128)(2,1)S(1)} %collective-permute-done.2.refs_1_), channel_id=1, source_target_pairs={{0,480},{32,0},{64,32},{96,64},{128,96},{160,128},{192,160},{224,1... | collective-permute-start | bytes 884744 | tf_op jit(solution)/shard_map/ppermute | solution.py:395
  69.4 6.1 %collective-permute-done.9.refs_14_ = bf16[192,768]{1,0:T(8,128)(2,1)S(1)} collective-permute-done((bf16[192,768]{1,0:T(8,128)(2,1)S(1)}, bf16[192,768]{1,0:T(8,128)(2,1)S(1)}, u32[]{:S(2)}, u32[]{:S(2)}) %collective-permute-start.9) | collective-permute-done | bytes 294944 | tf_op jit(solution)/shard_map/ppermute | solution.py:392
  77.5 4.6 %collective-permute-start.17 = (bf16[192,768]{1,0:T(8,128)(2,1)S(1)}, bf16[192,768]{1,0:T(8,128)(2,1)S(1)}, u32[]{:S(2)}, u32[]{:S(2)}) collective-permute-start(bf16[192,768]{1,0:T(8,128)(2,1)S(1)} %collective-permute-done.16.refs_18_), channel_id=1, source_target_pairs={{0,480},{32,0},{64,32},{96,64},{128,96},{160,128},{192,160},{224,1... | collective-permute-start | bytes 884744 | tf_op jit(solution)/shard_map/ppermute | solution.py:393
  82.1 6.1 %collective-permute-done.24.refs_30_ = bf16[192,768]{1,0:T(8,128)(2,1)S(1)} collective-permute-done((bf16[192,768]{1,0:T(8,128)(2,1)S(1)}, bf16[192,768]{1,0:T(8,128)(2,1)S(1)}, u32[]{:S(2)}, u32[]{:S(2)}) %collective-permute-start.24) | collective-permute-done | bytes 294944 | tf_op jit(solution)/shard_map/ppermute | solution.py:396
  90.2 4.6 %collective-permute-start.4 = (bf16[192,768]{1,0:T(8,128)(2,1)S(1)}, bf16[192,768]{1,0:T(8,128)(2,1)S(1)}, u32[]{:S(2)}, u32[]{:S(2)}) collective-permute-start(bf16[192,768]{1,0:T(8,128)(2,1)S(1)} %collective-permute-done.3.refs_2_), channel_id=1, source_target_pairs={{0,480},{32,0},{64,32},{96,64},{128,96},{160,128},{192,160},{224,1... | collective-permute-start | bytes 884744 | tf_op jit(solution)/shard_map/ppermute | solution.py:395
  94.7 6.1 %collective-permute-done.10.refs_13_ = bf16[192,768]{1,0:T(8,128)(2,1)S(1)} collective-permute-done((bf16[192,768]{1,0:T(8,128)(2,1)S(1)}, bf16[192,768]{1,0:T(8,128)(2,1)S(1)}, u32[]{:S(2)}, u32[]{:S(2)}) %collective-permute-start.10) | collective-permute-done | bytes 294944 | tf_op jit(solution)/shard_map/ppermute | solution.py:392
  107.4 6.1 %collective-permute-done.25.refs_29_ = bf16[192,768]{1,0:T(8,128)(2,1)S(1)} collective-permute-done((bf16[192,768]{1,0:T(8,128)(2,1)S(1)}, bf16[192,768]{1,0:T(8,128)(2,1)S(1)}, u32[]{:S(2)}, u32[]{:S(2)}) %collective-permute-start.25) | collective-permute-done | bytes 294944 | tf_op jit(solution)/shard_map/ppermute | solution.py:396
  120.0 6.1 %collective-permute-done.11.refs_12_ = bf16[192,768]{1,0:T(8,128)(2,1)S(1)} collective-permute-done((bf16[192,768]{1,0:T(8,128)(2,1)S(1)}, bf16[192,768]{1,0:T(8,128)(2,1)S(1)}, u32[]{:S(2)}, u32[]{:S(2)}) %collective-permute-start.11) | collective-permute-done | bytes 294944 | tf_op jit(solution)/shard_map/ppermute | solution.py:392
  128.1 4.6 %collective-permute-start.19 = (bf16[192,768]{1,0:T(8,128)(2,1)S(1)}, bf16[192,768]{1,0:T(8,128)(2,1)S(1)}, u32[]{:S(2)}, u32[]{:S(2)}) collective-permute-start(bf16[192,768]{1,0:T(8,128)(2,1)S(1)} %collective-permute-done.18.refs_20_), channel_id=1, source_target_pairs={{0,480},{32,0},{64,32},{96,64},{128,96},{160,128},{192,160},{224,1... | collective-permute-start | bytes 884744 | tf_op jit(solution)/shard_map/ppermute | solution.py:393
  132.7 6.1 %collective-permute-done.26.refs_28_ = bf16[192,768]{1,0:T(8,128)(2,1)S(1)} collective-permute-done((bf16[192,768]{1,0:T(8,128)(2,1)S(1)}, bf16[192,768]{1,0:T(8,128)(2,1)S(1)}, u32[]{:S(2)}, u32[]{:S(2)}) %collective-permute-start.26) | collective-permute-done | bytes 294944 | tf_op jit(solution)/shard_map/ppermute | solution.py:396
  140.7 4.6 %collective-permute-start.6 = (bf16[192,768]{1,0:T(8,128)(2,1)S(1)}, bf16[192,768]{1,0:T(8,128)(2,1)S(1)}, u32[]{:S(2)}, u32[]{:S(2)}) collective-permute-start(bf16[192,768]{1,0:T(8,128)(2,1)S(1)} %collective-permute-done.5.refs_4_), channel_id=1, source_target_pairs={{0,480},{32,0},{64,32},{96,64},{128,96},{160,128},{192,160},{224,1... | collective-permute-start | bytes 884744 | tf_op jit(solution)/shard_map/ppermute | solution.py:395
  145.3 6.1 %collective-permute-done.12.refs_11_ = bf16[192,768]{1,0:T(8,128)(2,1)S(1)} collective-permute-done((bf16[192,768]{1,0:T(8,128)(2,1)S(1)}, bf16[192,768]{1,0:T(8,128)(2,1)S(1)}, u32[]{:S(2)}, u32[]{:S(2)}) %collective-permute-start.12) | collective-permute-done | bytes 294944 | tf_op jit(solution)/shard_map/ppermute | solution.py:392
  153.4 4.6 %collective-permute-start.20 = (bf16[192,768]{1,0:T(8,128)(2,1)S(1)}, bf16[192,768]{1,0:T(8,128)(2,1)S(1)}, u32[]{:S(2)}, u32[]{:S(2)}) collective-permute-start(bf16[192,768]{1,0:T(8,128)(2,1)S(1)} %collective-permute-done.19.refs_21_), channel_id=1, source_target_pairs={{0,480},{32,0},{64,32},{96,64},{128,96},{160,128},{192,160},{224,1... | collective-permute-start | bytes 884744 | tf_op jit(solution)/shard_map/ppermute | solution.py:393
  157.9 6.1 %collective-permute-done.27.refs_27_ = bf16[192,768]{1,0:T(8,128)(2,1)S(1)} collective-permute-done((bf16[192,768]{1,0:T(8,128)(2,1)S(1)}, bf16[192,768]{1,0:T(8,128)(2,1)S(1)}, u32[]{:S(2)}, u32[]{:S(2)}) %collective-permute-start.27) | collective-permute-done | bytes 294944 | tf_op jit(solution)/shard_map/ppermute | solution.py:396
  166.0 4.6 %collective-permute-start.7 = (bf16[192,768]{1,0:T(8,128)(2,1)S(1)}, bf16[192,768]{1,0:T(8,128)(2,1)}, u32[]{:S(2)}, u32[]{:S(2)}) collective-permute-start(bf16[192,768]{1,0:T(8,128)(2,1)S(1)} %collective-permute-done.6.refs_5_), channel_id=1, source_target_pairs={{0,480},{32,0},{64,32},{96,64},{128,96},{160,128},{192,160},{224,1... | collective-permute-start | bytes 884744 | tf_op jit(solution)/shard_map/ppermute | solution.py:395
  170.6 6.1 %collective-permute-done.13.refs_10_ = bf16[192,768]{1,0:T(8,128)(2,1)S(1)} collective-permute-done((bf16[192,768]{1,0:T(8,128)(2,1)S(1)}, bf16[192,768]{1,0:T(8,128)(2,1)S(1)}, u32[]{:S(2)}, u32[]{:S(2)}) %collective-permute-start.13) | collective-permute-done | bytes 294944 | tf_op jit(solution)/shard_map/ppermute | solution.py:392
  178.6 4.6 %collective-permute-start.21 = (bf16[192,768]{1,0:T(8,128)(2,1)S(1)}, bf16[192,768]{1,0:T(8,128)(2,1)}, u32[]{:S(2)}, u32[]{:S(2)}) collective-permute-start(bf16[192,768]{1,0:T(8,128)(2,1)S(1)} %collective-permute-done.20.refs_22_), channel_id=1, source_target_pairs={{0,480},{32,0},{64,32},{96,64},{128,96},{160,128},{192,160},{224,1... | collective-permute-start | bytes 884744 | tf_op jit(solution)/shard_map/ppermute | solution.py:393
  183.2 6.1 %collective-permute-done.28.refs_26_ = bf16[192,768]{1,0:T(8,128)(2,1)} collective-permute-done((bf16[192,768]{1,0:T(8,128)(2,1)S(1)}, bf16[192,768]{1,0:T(8,128)(2,1)}, u32[]{:S(2)}, u32[]{:S(2)}) %collective-permute-start.28) | collective-permute-done | bytes 294944 | tf_op jit(solution)/shard_map/ppermute | solution.py:396
  191.3 4.6 %collective-permute-start.8 = (bf16[192,768]{1,0:T(8,128)(2,1)}, bf16[192,768]{1,0:T(8,128)(2,1)}, u32[]{:S(2)}, u32[]{:S(2)}) collective-permute-start(bf16[192,768]{1,0:T(8,128)(2,1)} %collective-permute-done.7.refs_6_), channel_id=1, source_target_pairs={{0,480},{32,0},{64,32},{96,64},{128,96},{160,128},{192,160},{224,1... | collective-permute-start | bytes 884744 | tf_op jit(solution)/shard_map/ppermute | solution.py:395
  195.9 6.1 %collective-permute-done.14.refs_9_ = bf16[192,768]{1,0:T(8,128)(2,1)} collective-permute-done((bf16[192,768]{1,0:T(8,128)(2,1)S(1)}, bf16[192,768]{1,0:T(8,128)(2,1)}, u32[]{:S(2)}, u32[]{:S(2)}) %collective-permute-start.14) | collective-permute-done | bytes 294944 | tf_op jit(solution)/shard_map/ppermute | solution.py:392
  203.9 4.6 %collective-permute-start.22 = (bf16[192,768]{1,0:T(8,128)(2,1)}, bf16[192,768]{1,0:T(8,128)(2,1)}, u32[]{:S(2)}, u32[]{:S(2)}) collective-permute-start(bf16[192,768]{1,0:T(8,128)(2,1)} %collective-permute-done.21.refs_23_), channel_id=1, source_target_pairs={{0,480},{32,0},{64,32},{96,64},{128,96},{160,128},{192,160},{224,1... | collective-permute-start | bytes 884744 | tf_op jit(solution)/shard_map/ppermute | solution.py:393
  210.0 5.3 %shard_map.102.x = bf16[2,320,2048]{2,1,0:T(8,128)(2,1)} custom-call(bf16[512,2560]{1,0:T(8,128)(2,1)} %bitcast.21), custom_call_target="tpu_custom_call" | custom-call | flops 1342177280 | bytes 6291456 | tf_op jit(solution)/shard_map/pallas_call | solution.py:300
  219.0 10.4 %shard_map.103 = bf16[256,2560]{1,0:T(8,128)(2,1)} custom-call(s32[1]{0:T(128)} %bitcast.13.me, bf16[2,320,2048]{2,1,0:T(8,128)(2,1)} %shard_map.102.x, bf16[192,768]{1,0:T(8,128)(2,1)} %get-tuple-element.15.refs_0_, bf16[192,768]{1,0:T(8,128)(2,1)} %copy-done.8, bf16[192,768]{1,0:T(8,128)(2,1)} %copy-done.12, bf16[192,768]{1,0:T(8,128)(2,1)} %copy-done.16, ...), custom_call_target="tpu_custom_call" | custom-call | flops 3019898880 | bytes 13631488 | tf_op jit(solution)/shard_map/pallas_call | solution.py:336
  229.4 7.5 %all-to-all-start.2 = ((bf16[32,8,2560]{2,1,0:T(8,128)(2,1)}), bf16[32,8,2560]{2,1,0:T(8,128)(2,1)S(1)}, u32[]{:S(2)}, u32[]{:S(2)}) async-start(bf16[32,8,2560]{2,1,0:T(8,128)(2,1)} %bitcast.26), calls=%async_computation.2 | async-start | bytes 2621440 | tf_op jit(solution)/shard_map/all_to_all | solution.py:372
  236.9 8.0 %shard_map.104 = bf16[256,2560]{1,0:T(8,128)(2,1)} custom-call(bf16[2,320,2048]{2,1,0:T(8,128)(2,1)} %shard_map.102.x, bf16[16,384,768]{2,1,0:T(8,128)(2,1)} %bitcast.22), custom_call_target="tpu_custom_call" | custom-call | flops 3019898880 | bytes 13631488 | tf_op jit(solution)/shard_map/pallas_call | solution.py:319
  244.9 11.7 %all-to-all-done.2 = bf16[32,8,2560]{2,1,0:T(8,128)(2,1)S(1)} async-done(((bf16[32,8,2560]{2,1,0:T(8,128)(2,1)}), bf16[32,8,2560]{2,1,0:T(8,128)(2,1)S(1)}, u32[]{:S(2)}, u32[]{:S(2)}) %all-to-all-start.2) | async-done | bytes 1310752 | tf_op jit(solution)/shard_map/all_to_all | solution.py:372
  263.8 16.7 %all-to-all-done.1 = bf16[32,8,2560]{2,1,0:T(8,128)(2,1)S(1)} async-done(((bf16[32,8,2560]{2,1,0:T(8,128)(2,1)}), bf16[32,8,2560]{2,1,0:T(8,128)(2,1)S(1)}, u32[]{:S(2)}, u32[]{:S(2)}) %all-to-all-start.1) | async-done | bytes 1310752 | tf_op jit(solution)/shard_map/all_to_all | solution.py:372
  (109 shorter events, 71.8 us)
Async XLA Ops:
  6.5 230.4 %all-gather.3.cloned.1.call-start = ((), (), s32[]{:S(2)}) async-start(), calls=%async_computation.3 | async-start | bytes 10027008 | tf_op jit(solution)/shard_map/all_gather | solution.py:388
  8.9 21.6 %collective-permute-start = (bf16[192,768]{1,0:T(8,128)(2,1)}, bf16[192,768]{1,0:T(8,128)(2,1)S(1)}, u32[]{:S(2)}, u32[]{:S(2)}) collective-permute-start(bf16[192,768]{1,0:T(8,128)(2,1)} %get-tuple-element.15.refs_0_), channel_id=1, source_target_pairs={{0,32},{32,64},{64,96},{96,128},{128,160},{160,192},{192,224},{224... | collective-permute-start | bytes 884744 | tf_op jit(solution)/shard_map/ppermute | solution.py:392
  13.3 17.3 %collective-permute-start.1 = (bf16[192,768]{1,0:T(8,128)(2,1)}, bf16[192,768]{1,0:T(8,128)(2,1)S(1)}, u32[]{:S(2)}, u32[]{:S(2)}) collective-permute-start(bf16[192,768]{1,0:T(8,128)(2,1)} %get-tuple-element.16.refs_16_), channel_id=1, source_target_pairs={{0,480},{32,0},{64,32},{96,64},{128,96},{160,128},{192,160},{224,1... | collective-permute-start | bytes 884744 | tf_op jit(solution)/shard_map/ppermute | solution.py:393
  36.5 172.0 %all-to-all-start = ((bf16[32,16,2560]{2,1,0:T(8,128)(2,1)}), bf16[32,16,2560]{2,1,0:T(8,128)(2,1)S(1)}, u32[]{:S(2)}, u32[]{:S(2)}) async-start(bf16[32,16,2560]{2,1,0:T(8,128)(2,1)} %bitcast.27), calls=%async_computation | async-start | bytes 5242880 | tf_op jit(solution)/shard_map/all_to_all | solution.py:372
  44.6 18.3 %collective-permute-start.23 = (bf16[192,768]{1,0:T(8,128)(2,1)S(1)}, bf16[192,768]{1,0:T(8,128)(2,1)S(1)}, u32[]{:S(2)}, u32[]{:S(2)}) collective-permute-start(bf16[192,768]{1,0:T(8,128)(2,1)S(1)} %copy-done.4), channel_id=1, source_target_pairs={{0,32},{32,64},{64,96},{96,128},{128,160},{160,192},{192,224},{224... | collective-permute-start | bytes 884744 | tf_op jit(solution)/shard_map/ppermute | solution.py:396
  46.6 18.3 %collective-permute-start.2 = (bf16[192,768]{1,0:T(8,128)(2,1)S(1)}, bf16[192,768]{1,0:T(8,128)(2,1)S(1)}, u32[]{:S(2)}, u32[]{:S(2)}) collective-permute-start(bf16[192,768]{1,0:T(8,128)(2,1)S(1)} %copy-done.3), channel_id=1, source_target_pairs={{0,480},{32,0},{64,32},{96,64},{128,96},{160,128},{192,160},{224,1... | collective-permute-start | bytes 884744 | tf_op jit(solution)/shard_map/ppermute | solution.py:395
  51.2 24.4 %collective-permute-start.9 = (bf16[192,768]{1,0:T(8,128)(2,1)S(1)}, bf16[192,768]{1,0:T(8,128)(2,1)S(1)}, u32[]{:S(2)}, u32[]{:S(2)}) collective-permute-start(bf16[192,768]{1,0:T(8,128)(2,1)S(1)} %collective-permute-done.refs_15_), channel_id=1, source_target_pairs={{0,32},{32,64},{64,96},{96,128},{128,160},{160,192},{192,224},{224... | collective-permute-start | bytes 884744 | tf_op jit(solution)/shard_map/ppermute | solution.py:392
  53.1 24.4 %collective-permute-start.16 = (bf16[192,768]{1,0:T(8,128)(2,1)}, bf16[192,768]{1,0:T(8,128)(2,1)S(1)}, u32[]{:S(2)}, u32[]{:S(2)}) collective-permute-start(bf16[192,768]{1,0:T(8,128)(2,1)} %copy-done.6), channel_id=1, source_target_pairs={{0,480},{32,0},{64,32},{96,64},{128,96},{160,128},{192,160},{224,1... | collective-permute-start | bytes 884744 | tf_op jit(solution)/shard_map/ppermute | solution.py:393
  62.9 25.3 %collective-permute-start.24 = (bf16[192,768]{1,0:T(8,128)(2,1)S(1)}, bf16[192,768]{1,0:T(8,128)(2,1)S(1)}, u32[]{:S(2)}, u32[]{:S(2)}) collective-permute-start(bf16[192,768]{1,0:T(8,128)(2,1)S(1)} %collective-permute-done.23.refs_31_), channel_id=1, source_target_pairs={{0,32},{32,64},{64,96},{96,128},{128,160},{160,192},{192,224},{224... | collective-permute-start | bytes 884744 | tf_op jit(solution)/shard_map/ppermute | solution.py:396
  64.9 25.3 %collective-permute-start.3 = (bf16[192,768]{1,0:T(8,128)(2,1)S(1)}, bf16[192,768]{1,0:T(8,128)(2,1)S(1)}, u32[]{:S(2)}, u32[]{:S(2)}) collective-permute-start(bf16[192,768]{1,0:T(8,128)(2,1)S(1)} %collective-permute-done.2.refs_1_), channel_id=1, source_target_pairs={{0,480},{32,0},{64,32},{96,64},{128,96},{160,128},{192,160},{224,1... | collective-permute-start | bytes 884744 | tf_op jit(solution)/shard_map/ppermute | solution.py:395
  75.6 25.3 %collective-permute-start.10 = (bf16[192,768]{1,0:T(8,128)(2,1)S(1)}, bf16[192,768]{1,0:T(8,128)(2,1)S(1)}, u32[]{:S(2)}, u32[]{:S(2)}) collective-permute-start(bf16[192,768]{1,0:T(8,128)(2,1)S(1)} %collective-permute-done.9.refs_14_), channel_id=1, source_target_pairs={{0,32},{32,64},{64,96},{96,128},{128,160},{160,192},{192,224},{224... | collective-permute-start | bytes 884744 | tf_op jit(solution)/shard_map/ppermute | solution.py:392
  77.5 25.3 %collective-permute-start.17 = (bf16[192,768]{1,0:T(8,128)(2,1)S(1)}, bf16[192,768]{1,0:T(8,128)(2,1)S(1)}, u32[]{:S(2)}, u32[]{:S(2)}) collective-permute-start(bf16[192,768]{1,0:T(8,128)(2,1)S(1)} %collective-permute-done.16.refs_18_), channel_id=1, source_target_pairs={{0,480},{32,0},{64,32},{96,64},{128,96},{160,128},{192,160},{224,1... | collective-permute-start | bytes 884744 | tf_op jit(solution)/shard_map/ppermute | solution.py:393
  88.2 25.3 %collective-permute-start.25 = (bf16[192,768]{1,0:T(8,128)(2,1)S(1)}, bf16[192,768]{1,0:T(8,128)(2,1)S(1)}, u32[]{:S(2)}, u32[]{:S(2)}) collective-permute-start(bf16[192,768]{1,0:T(8,128)(2,1)S(1)} %collective-permute-done.24.refs_30_), channel_id=1, source_target_pairs={{0,32},{32,64},{64,96},{96,128},{128,160},{160,192},{192,224},{224... | collective-permute-start | bytes 884744 | tf_op jit(solution)/shard_map/ppermute | solution.py:396
  90.2 25.2 %collective-permute-start.4 = (bf16[192,768]{1,0:T(8,128)(2,1)S(1)}, bf16[192,768]{1,0:T(8,128)(2,1)S(1)}, u32[]{:S(2)}, u32[]{:S(2)}) collective-permute-start(bf16[192,768]{1,0:T(8,128)(2,1)S(1)} %collective-permute-done.3.refs_2_), channel_id=1, source_target_pairs={{0,480},{32,0},{64,32},{96,64},{128,96},{160,128},{192,160},{224,1... | collective-permute-start | bytes 884744 | tf_op jit(solution)/shard_map/ppermute | solution.py:395
  100.9 25.3 %collective-permute-start.11 = (bf16[192,768]{1,0:T(8,128)(2,1)S(1)}, bf16[192,768]{1,0:T(8,128)(2,1)S(1)}, u32[]{:S(2)}, u32[]{:S(2)}) collective-permute-start(bf16[192,768]{1,0:T(8,128)(2,1)S(1)} %collective-permute-done.10.refs_13_), channel_id=1, source_target_pairs={{0,32},{32,64},{64,96},{96,128},{128,160},{160,192},{192,224},{224... | collective-permute-start | bytes 884744 | tf_op jit(solution)/shard_map/ppermute | solution.py:392
  102.8 25.3 %collective-permute-start.18 = (bf16[192,768]{1,0:T(8,128)(2,1)S(1)}, bf16[192,768]{1,0:T(8,128)(2,1)S(1)}, u32[]{:S(2)}, u32[]{:S(2)}) collective-permute-start(bf16[192,768]{1,0:T(8,128)(2,1)S(1)} %collective-permute-done.17.refs_19_), channel_id=1, source_target_pairs={{0,480},{32,0},{64,32},{96,64},{128,96},{160,128},{192,160},{224,1... | collective-permute-start | bytes 884744 | tf_op jit(solution)/shard_map/ppermute | solution.py:393
  113.5 25.3 %collective-permute-start.26 = (bf16[192,768]{1,0:T(8,128)(2,1)S(1)}, bf16[192,768]{1,0:T(8,128)(2,1)S(1)}, u32[]{:S(2)}, u32[]{:S(2)}) collective-permute-start(bf16[192,768]{1,0:T(8,128)(2,1)S(1)} %collective-permute-done.25.refs_29_), channel_id=1, source_target_pairs={{0,32},{32,64},{64,96},{96,128},{128,160},{160,192},{192,224},{224... | collective-permute-start | bytes 884744 | tf_op jit(solution)/shard_map/ppermute | solution.py:396
  115.4 25.3 %collective-permute-start.5 = (bf16[192,768]{1,0:T(8,128)(2,1)S(1)}, bf16[192,768]{1,0:T(8,128)(2,1)S(1)}, u32[]{:S(2)}, u32[]{:S(2)}) collective-permute-start(bf16[192,768]{1,0:T(8,128)(2,1)S(1)} %collective-permute-done.4.refs_3_), channel_id=1, source_target_pairs={{0,480},{32,0},{64,32},{96,64},{128,96},{160,128},{192,160},{224,1... | collective-permute-start | bytes 884744 | tf_op jit(solution)/shard_map/ppermute | solution.py:395
  126.1 25.3 %collective-permute-start.12 = (bf16[192,768]{1,0:T(8,128)(2,1)S(1)}, bf16[192,768]{1,0:T(8,128)(2,1)S(1)}, u32[]{:S(2)}, u32[]{:S(2)}) collective-permute-start(bf16[192,768]{1,0:T(8,128)(2,1)S(1)} %collective-permute-done.11.refs_12_), channel_id=1, source_target_pairs={{0,32},{32,64},{64,96},{96,128},{128,160},{160,192},{192,224},{224... | collective-permute-start | bytes 884744 | tf_op jit(solution)/shard_map/ppermute | solution.py:392
  128.1 25.3 %collective-permute-start.19 = (bf16[192,768]{1,0:T(8,128)(2,1)S(1)}, bf16[192,768]{1,0:T(8,128)(2,1)S(1)}, u32[]{:S(2)}, u32[]{:S(2)}) collective-permute-start(bf16[192,768]{1,0:T(8,128)(2,1)S(1)} %collective-permute-done.18.refs_20_), channel_id=1, source_target_pairs={{0,480},{32,0},{64,32},{96,64},{128,96},{160,128},{192,160},{224,1... | collective-permute-start | bytes 884744 | tf_op jit(solution)/shard_map/ppermute | solution.py:393
  138.8 25.3 %collective-permute-start.27 = (bf16[192,768]{1,0:T(8,128)(2,1)S(1)}, bf16[192,768]{1,0:T(8,128)(2,1)S(1)}, u32[]{:S(2)}, u32[]{:S(2)}) collective-permute-start(bf16[192,768]{1,0:T(8,128)(2,1)S(1)} %collective-permute-done.26.refs_28_), channel_id=1, source_target_pairs={{0,32},{32,64},{64,96},{96,128},{128,160},{160,192},{192,224},{224... | collective-permute-start | bytes 884744 | tf_op jit(solution)/shard_map/ppermute | solution.py:396
  140.7 25.3 %collective-permute-start.6 = (bf16[192,768]{1,0:T(8,128)(2,1)S(1)}, bf16[192,768]{1,0:T(8,128)(2,1)S(1)}, u32[]{:S(2)}, u32[]{:S(2)}) collective-permute-start(bf16[192,768]{1,0:T(8,128)(2,1)S(1)} %collective-permute-done.5.refs_4_), channel_id=1, source_target_pairs={{0,480},{32,0},{64,32},{96,64},{128,96},{160,128},{192,160},{224,1... | collective-permute-start | bytes 884744 | tf_op jit(solution)/shard_map/ppermute | solution.py:395
  151.4 25.3 %collective-permute-start.13 = (bf16[192,768]{1,0:T(8,128)(2,1)S(1)}, bf16[192,768]{1,0:T(8,128)(2,1)S(1)}, u32[]{:S(2)}, u32[]{:S(2)}) collective-permute-start(bf16[192,768]{1,0:T(8,128)(2,1)S(1)} %collective-permute-done.12.refs_11_), channel_id=1, source_target_pairs={{0,32},{32,64},{64,96},{96,128},{128,160},{160,192},{192,224},{224... | collective-permute-start | bytes 884744 | tf_op jit(solution)/shard_map/ppermute | solution.py:392
  153.4 25.3 %collective-permute-start.20 = (bf16[192,768]{1,0:T(8,128)(2,1)S(1)}, bf16[192,768]{1,0:T(8,128)(2,1)S(1)}, u32[]{:S(2)}, u32[]{:S(2)}) collective-permute-start(bf16[192,768]{1,0:T(8,128)(2,1)S(1)} %collective-permute-done.19.refs_21_), channel_id=1, source_target_pairs={{0,480},{32,0},{64,32},{96,64},{128,96},{160,128},{192,160},{224,1... | collective-permute-start | bytes 884744 | tf_op jit(solution)/shard_map/ppermute | solution.py:393
  164.1 25.3 %collective-permute-start.28 = (bf16[192,768]{1,0:T(8,128)(2,1)S(1)}, bf16[192,768]{1,0:T(8,128)(2,1)}, u32[]{:S(2)}, u32[]{:S(2)}) collective-permute-start(bf16[192,768]{1,0:T(8,128)(2,1)S(1)} %collective-permute-done.27.refs_27_), channel_id=1, source_target_pairs={{0,32},{32,64},{64,96},{96,128},{128,160},{160,192},{192,224},{224... | collective-permute-start | bytes 884744 | tf_op jit(solution)/shard_map/ppermute | solution.py:396
  166.0 25.2 %collective-permute-start.7 = (bf16[192,768]{1,0:T(8,128)(2,1)S(1)}, bf16[192,768]{1,0:T(8,128)(2,1)}, u32[]{:S(2)}, u32[]{:S(2)}) collective-permute-start(bf16[192,768]{1,0:T(8,128)(2,1)S(1)} %collective-permute-done.6.refs_5_), channel_id=1, source_target_pairs={{0,480},{32,0},{64,32},{96,64},{128,96},{160,128},{192,160},{224,1... | collective-permute-start | bytes 884744 | tf_op jit(solution)/shard_map/ppermute | solution.py:395
  176.7 25.3 %collective-permute-start.14 = (bf16[192,768]{1,0:T(8,128)(2,1)S(1)}, bf16[192,768]{1,0:T(8,128)(2,1)}, u32[]{:S(2)}, u32[]{:S(2)}) collective-permute-start(bf16[192,768]{1,0:T(8,128)(2,1)S(1)} %collective-permute-done.13.refs_10_), channel_id=1, source_target_pairs={{0,32},{32,64},{64,96},{96,128},{128,160},{160,192},{192,224},{224... | collective-permute-start | bytes 884744 | tf_op jit(solution)/shard_map/ppermute | solution.py:392
  178.6 25.2 %collective-permute-start.21 = (bf16[192,768]{1,0:T(8,128)(2,1)S(1)}, bf16[192,768]{1,0:T(8,128)(2,1)}, u32[]{:S(2)}, u32[]{:S(2)}) collective-permute-start(bf16[192,768]{1,0:T(8,128)(2,1)S(1)} %collective-permute-done.20.refs_22_), channel_id=1, source_target_pairs={{0,480},{32,0},{64,32},{96,64},{128,96},{160,128},{192,160},{224,1... | collective-permute-start | bytes 884744 | tf_op jit(solution)/shard_map/ppermute | solution.py:393
  189.3 25.9 %collective-permute-start.29 = (bf16[192,768]{1,0:T(8,128)(2,1)}, bf16[192,768]{1,0:T(8,128)(2,1)}, u32[]{:S(2)}, u32[]{:S(2)}) collective-permute-start(bf16[192,768]{1,0:T(8,128)(2,1)} %collective-permute-done.28.refs_26_), channel_id=1, source_target_pairs={{0,32},{32,64},{64,96},{96,128},{128,160},{160,192},{192,224},{224... | collective-permute-start | bytes 884744 | tf_op jit(solution)/shard_map/ppermute | solution.py:396
  191.3 24.0 %collective-permute-start.8 = (bf16[192,768]{1,0:T(8,128)(2,1)}, bf16[192,768]{1,0:T(8,128)(2,1)}, u32[]{:S(2)}, u32[]{:S(2)}) collective-permute-start(bf16[192,768]{1,0:T(8,128)(2,1)} %collective-permute-done.7.refs_6_), channel_id=1, source_target_pairs={{0,480},{32,0},{64,32},{96,64},{128,96},{160,128},{192,160},{224,1... | collective-permute-start | bytes 884744 | tf_op jit(solution)/shard_map/ppermute | solution.py:395
  229.4 27.3 %all-to-all-start.2 = ((bf16[32,8,2560]{2,1,0:T(8,128)(2,1)}), bf16[32,8,2560]{2,1,0:T(8,128)(2,1)S(1)}, u32[]{:S(2)}, u32[]{:S(2)}) async-start(bf16[32,8,2560]{2,1,0:T(8,128)(2,1)} %bitcast.26), calls=%async_computation.2 | async-start | bytes 2621440 | tf_op jit(solution)/shard_map/all_to_all | solution.py:372
  256.7 23.9 %all-to-all-start.1 = ((bf16[32,8,2560]{2,1,0:T(8,128)(2,1)}), bf16[32,8,2560]{2,1,0:T(8,128)(2,1)S(1)}, u32[]{:S(2)}, u32[]{:S(2)}) async-start(bf16[32,8,2560]{2,1,0:T(8,128)(2,1)} %bitcast.23), calls=%async_computation.1 | async-start | bytes 2621440 | tf_op jit(solution)/shard_map/all_to_all | solution.py:372
  (30 other events, 790.7 us)
Sparse Core Ops, SparseCore 0:
  9.4 201.4 all-gather.2

commit v2 on v1

--- a/solution.py
+++ b/solution.py
@@ -1,3 +1,5 @@
+import functools
+
 import jax
 import jax.numpy as jnp
 from jax import lax
@@ -9,6 +11,7 @@
 GROUP = 2
 LANE = 128
 VMEM_LIMIT = 56 * 1024 * 1024
+SMALL_LIMIT = 24 * 1024 * 1024
 
 TOK = 128
 CHOICES = TOK * TOP
@@ -24,6 +27,9 @@
 PIECES = 16
 PIECE = 3 * LANE
 HALF = PIECE // 2
+LAG = 0
+XSTEP = 6
+KSTEP = 4
 
 
 def iota(shape, axis):
@@ -150,14 +156,11 @@
             out[e, MAIN_E:, at] = dot(own, x[:, D:]).astype(jnp.bfloat16)
 
 
-def pack_kernel(gate, up, down, first, high, low):
-    first[:LANE, :] = gate[0]
-    first[LANE : 2 * LANE, :] = up[0]
-    first[2 * LANE :, :] = down[0].T
-    high[:LANE, :] = gate[1]
-    high[LANE:, :] = up[1, : HALF - LANE]
-    low[: HALF - LANE, :] = up[1, HALF - LANE :]
-    low[HALF - LANE :, :] = down[1].T
+def pack_kernel(gate, up, down, *outs):
+    for e, out in enumerate(outs):
+        out[:LANE, :] = gate[e]
+        out[LANE : 2 * LANE, :] = up[e]
+        out[2 * LANE :, :] = down[e].T
 
 
 WIDE = 2 * LANE
@@ -190,37 +193,27 @@
     out[:, D:] = packed.astype(jnp.bfloat16)
 
 
-def first_kernel(x, weights, out, gate_w, up_w, down_w, hidden_s, rows, sems, sem):
-    copies = [[pltpu.make_async_copy(x.at[0], rows, sem)]] + [[] for _ in range(TILES + 3)]
-    for n in range(TILES):
-        cut = pl.ds(n * WIDE, WIDE)
-        for i, to in enumerate((gate_w, up_w)):
-            source = weights.at[:, pl.ds(i * LANE, LANE), cut]
-            copies[n].append(pltpu.make_async_copy(source, to.at[:, :, cut], sems.at[i, n]))
-    for q in range(4):
-        own = pl.ds(q * 4, 4)
-        source = weights.at[own, pl.ds(2 * LANE, LANE)]
-        copies[TILES + q].append(pltpu.make_async_copy(source, down_w.at[own], sems.at[2, q]))
-    expert(rows, out, gate_w, up_w, down_w, hidden_s, copies)
-
-
-def second_kernel(me, x, *refs):
-    highs, lows = refs[:PIECES], refs[PIECES : 2 * PIECES]
-    out, gate_w, up_w, down_w, hidden_s, sems = refs[2 * PIECES :]
-    copies = [[] for _ in range(TILES + 4)]
+def expert_kernel(e, me, x, *refs):
+    pieces, high, low = refs[: PIECES - 1], refs[PIECES - 1], refs[PIECES]
+    out, gate_w, up_w, down_w, hidden_s, rows, sems, sem = refs[PIECES + 1 :]
+    copies = [[pltpu.make_async_copy(x.at[e], rows, sem)]] + [[] for _ in range(TILES + 3)]
     half = HALF - LANE
     for j in range(PIECES):
         owner = lax.rem(me[0] + j, PIECES)
-        moves = [
-            (highs[j].at[pl.ds(0, LANE)], gate_w.at[owner]),
-            (highs[j].at[pl.ds(LANE, half)], up_w.at[owner, pl.ds(0, half)]),
-            (lows[j].at[pl.ds(0, half)], up_w.at[owner, pl.ds(half, half)]),
-            (lows[j].at[pl.ds(half, LANE)], down_w.at[owner]),
-        ]
+        if j == PIECES // 2:
+            moves = [
+                (high.at[pl.ds(0, LANE)], gate_w.at[owner]),
+                (high.at[pl.ds(LANE, half)], up_w.at[owner, pl.ds(0, half)]),
+                (low.at[pl.ds(0, half)], up_w.at[owner, pl.ds(half, half)]),
+                (low.at[pl.ds(half, LANE)], down_w.at[owner]),
+            ]
+        else:
+            piece = pieces[j if j < PIECES // 2 else j - 1]
+            moves = [(piece.at[pl.ds(i * LANE, LANE)], to.at[owner]) for i, to in enumerate((gate_w, up_w, down_w))]
         now = [pltpu.make_async_copy(source, to, sems.at[i, j]) for i, (source, to) in enumerate(moves)]
         copies[0] += now[:-1]
         copies[TILES] += now[-1:]
-    expert(x.at[1], out, gate_w, up_w, down_w, hidden_s, copies)
+    expert(rows, out, gate_w, up_w, down_w, hidden_s, copies)
 
 
 def mix(e, ans, s_hi, s_lo, p_hi, p_lo):
@@ -238,16 +231,13 @@
     return total + jnp.concatenate(sums, axis=1)
 
 
-def mix_kernel(ans, s_hi, s_lo, p_hi, p_lo, out):
-    out[...] = mix(1, ans, s_hi, s_lo, p_hi, p_lo)
-
-
-def final_kernel(ans, s_hi, s_lo, p_hi, p_lo, before, out):
-    out[...] = (before[...] + mix(0, ans, s_hi, s_lo, p_hi, p_lo)).astype(jnp.bfloat16)
-
-
-def params():
-    return pltpu.CompilerParams(vmem_limit_bytes=VMEM_LIMIT)
+def final_kernel(first, second, s_hi, s_lo, p_hi, p_lo, out):
+    scales = (s_hi, s_lo, p_hi, p_lo)
+    out[...] = (mix(0, first, *scales) + mix(1, second, *scales)).astype(jnp.bfloat16)
+
+
+def params(size=SMALL_LIMIT):
+    return pltpu.CompilerParams(vmem_limit_bytes=size)
 
 
 def vmem(count):
@@ -285,13 +275,13 @@
 
 
 def pack(gate_weight, up_weight, down_weight):
-    half = jax.ShapeDtypeStruct((HALF, HID), jnp.bfloat16)
+    part = jax.ShapeDtypeStruct((PIECE, HID), jnp.bfloat16)
     return pl.pallas_call(
         pack_kernel,
-        out_shape=[jax.ShapeDtypeStruct((PIECE, HID), jnp.bfloat16), half, half],
+        out_shape=[part, part],
         in_specs=vmem(3),
-        out_specs=vmem(3),
-        compiler_params=params(),
+        out_specs=vmem(2),
+        compiler_params=params(VMEM_LIMIT),
         cost_estimate=cost(0, 8 * PIECE * HID),
     )(gate_weight, up_weight, down_weight)
 
@@ -307,63 +297,33 @@
     )(x)
 
 
-def expert_scratch():
-    return [pltpu.VMEM((PIECES, LANE, HID), jnp.bfloat16)] * 3 + [pltpu.VMEM((ROWS_E, HID), jnp.bfloat16)]
-
-
-EXPERT_OUT = jax.ShapeDtypeStruct((MAIN_E, D + D // 4), jnp.bfloat16)
-EXPERT_COST = cost(6 * ROWS_E * D * HID, 13 * 1024 * 1024)
-
-
-def first_expert(x, weights):
-    return pl.pallas_call(
-        first_kernel,
-        out_shape=EXPERT_OUT,
-        in_specs=anywhere(2),
+def expert_answers(e, me, x, pieces):
+    return pl.pallas_call(
+        functools.partial(expert_kernel, e),
+        out_shape=jax.ShapeDtypeStruct((MAIN_E, D + D // 4), jnp.bfloat16),
+        in_specs=[SMEM] + anywhere(1 + len(pieces)),
         out_specs=vmem(1)[0],
-        scratch_shapes=[
-            *expert_scratch(),
+        scratch_shapes=[pltpu.VMEM((PIECES, LANE, HID), jnp.bfloat16)] * 3
+        + [
+            pltpu.VMEM((ROWS_E, HID), jnp.bfloat16),
             pltpu.VMEM((ROWS_E, D), jnp.bfloat16),
-            pltpu.SemaphoreType.DMA((3, 4)),
+            pltpu.SemaphoreType.DMA((4, PIECES)),
             pltpu.SemaphoreType.DMA,
         ],
-        compiler_params=params(),
-        cost_estimate=EXPERT_COST,
-    )(x, weights)
-
-
-def second_expert(me, x, pieces):
-    return pl.pallas_call(
-        second_kernel,
-        out_shape=EXPERT_OUT,
-        in_specs=[SMEM] + vmem(1) + anywhere(len(pieces)),
-        out_specs=vmem(1)[0],
-        scratch_shapes=[*expert_scratch(), pltpu.SemaphoreType.DMA((4, PIECES))],
-        compiler_params=params(),
-        cost_estimate=EXPERT_COST,
+        compiler_params=params(VMEM_LIMIT),
+        cost_estimate=cost(6 * ROWS_E * D * HID, 13 * 1024 * 1024),
     )(me, x, *pieces)
 
 
-def combine(ans, scales):
-    return pl.pallas_call(
-        mix_kernel,
-        out_shape=jax.ShapeDtypeStruct((TOK, D), jnp.float32),
-        in_specs=vmem(5),
-        out_specs=vmem(1)[0],
-        compiler_params=params(),
-        cost_estimate=cost(5 * TOK * MAIN_E * D, 3 * 1024 * 1024),
-    )(ans, *scales)
-
-
-def combine_last(ans, scales, before):
+def combine(first, second, scales):
     return pl.pallas_call(
         final_kernel,
         out_shape=jax.ShapeDtypeStruct((TOK, D), jnp.bfloat16),
         in_specs=vmem(6),
         out_specs=vmem(1)[0],
         compiler_params=params(),
-        cost_estimate=cost(5 * TOK * MAIN_E * D, 3 * 1024 * 1024),
-    )(ans, *scales, before)
+        cost_estimate=cost(5 * TOK * MAIN * D, 4 * 1024 * 1024),
+    )(first, second, *scales)
 
 
 def exchange(block):
@@ -384,25 +344,36 @@
     right = [(i, (i + 1) % PIECES) for i in range(PIECES)]
     left = [(i, (i - 1) % PIECES) for i in range(PIECES)]
 
-    own, high, low = pack(gate_weight, up_weight, down_weight)
-    weights = lax.all_gather(own, "fsdp")
-    highs, lows = {0: high}, {0: low}
+    ring = [{0: own} for own in pack(gate_weight, up_weight, down_weight)]
     half = PIECES // 2
-    for step in range(1, half + 1):
-        highs[PIECES - step] = lax.ppermute(highs[(PIECES - step + 1) % PIECES], "fsdp", right)
-        lows[step] = lax.ppermute(lows[step - 1], "fsdp", left)
-        if step < half:
-            highs[step] = lax.ppermute(highs[step - 1], "fsdp", left)
-            lows[PIECES - step] = lax.ppermute(lows[(PIECES - step + 1) % PIECES], "fsdp", right)
-    pieces = [highs[j] for j in range(PIECES)] + [lows[j] for j in range(PIECES)]
-
-    ready = after(tokens, highs[PIECES - 1], lows[1])
-    out, *scales = dispatch(expert_ids, priority, overflow_pick, partner, capacity, route_scale, ready)
-    x = split_rows(exchange(out))
-    second = second_expert(me, x, pieces)
-    first = first_expert(after(x, second), weights)
-    before = combine(exchange(second), scales)
-    return combine_last(exchange(first), scales, before)
+    for turn in range(1, half + LAG + 1):
+        for e in range(2):
+            step = turn - e * LAG
+            if not 1 <= step <= half:
+                continue
+            piece = ring[e]
+            near_r, near_l = piece[(PIECES - step + 1) % PIECES], piece[step - 1]
+            if e == 0 and step == KSTEP:
+                out, *scales = dispatch(
+                    expert_ids, priority, overflow_pick, partner, capacity, route_scale, after(tokens, near_r)
+                )
+                x = split_rows(exchange(out))
+            if e == 1 and step == XSTEP:
+                near_r, near_l = after(near_r, x), after(near_l, x)
+            if e == 1 and step == 1 and LAG:
+                near_r = after(near_r, ring[0][(PIECES - turn + 1) % PIECES])
+                near_l = after(near_l, ring[0][turn - 1])
+            if step < half:
+                piece[PIECES - step] = lax.ppermute(near_r, "fsdp", right)
+                piece[step] = lax.ppermute(near_l, "fsdp", left)
+            else:
+                high = lax.ppermute(near_r[:HALF], "fsdp", right)
+                low = lax.ppermute(near_l[HALF:], "fsdp", left)
+                piece[half] = (high, low)
+    pieces = [[piece[j] for j in range(PIECES) if j != half] + list(piece[half]) for piece in ring]
+
+    first, second = (exchange(expert_answers(e, me, x, pieces[e])) for e in range(2))
+    return combine(first, second, scales)
 
 
 def solution(mesh):

time: 293 us -> 285 us (0.973)
  blocking collectives: 0 us -> 29 us
  waiting for transfers between devices: 105 us -> 82.4 us
  between operations: 14 us -> 0.74 us
  starting transfers between devices: 124 us -> 134 us
  Pallas kernels: 38.5 us -> 29.5 us
    all_to_all x0 -> x1, blocking collectives: none -> 29 us  [exchange(): lax.all_to_all(shaped, 'expert', split_axis=0, concat_axis=0, tiled=True)]
    all_to_all x3 -> x2, waiting for transfers between devices: 28.5 us -> 0.01 us  [exchange(): lax.all_to_all(shaped, 'expert', split_axis=0, concat_axis=0, tiled=True)]
    ppermute x30 -> x32, starting transfers between devices: 105 us -> 112 us  [the longest x14 69.7 us: per_device(): piece[step] = lax.ppermute(near_l, 'fsdp', left)]
    ppermute x30 -> x32, waiting for transfers between devices: 76.2 us -> 82.4 us  [the longest x14 76.4 us: per_device(): piece[PIECES - step] = lax.ppermute(near_r, 'fsdp', right)]
    pallas_call x1, Pallas kernels: 5.29 us -> 2.04 us  [split_rows(): pl.pallas_call(split_kernel, out_shape=jax.ShapeDtypeStruct((2, ROWS_E, D...]
    pallas_call x1, Pallas kernels: 5.94 us -> 2.84 us  [dispatch(): pl.pallas_call(dispatch_kernel, out_shape=[jax.ShapeDtypeStruct((MAIN, D...]
    pallas_call x5 -> x4, Pallas kernels: 27.3 us -> 24.6 us  [the longest x2 20.2 us: expert_answers(): pl.pallas_call(functools.partial(expert_kernel, e), out_shape=jax.ShapeDt...]
    all_to_all x3 -> x2, starting transfers between devices: 19.6 us -> 22.2 us  [exchange(): lax.all_to_all(shaped, 'expert', split_axis=0, concat_axis=0, tiled=True)]
  transfers between devices with their start and end apart: 34 -> 34, of which waited for: 15 -> 15; matrix products, arithmetic and copies ran while one was open for 3% -> 1% of each run, Pallas kernels for 11% -> 9%
where the time goes in v2:
time: 285 us; the launch traced here: 284 us
  starting transfers between devices  134 us (47%)
  waiting for transfers between devices  82.4 us (29%)
  Pallas kernels  29.5 us (10%)
  blocking collectives  29 us (10%)
  local copies, waits for them, and re-layouts  6.83 us (2%)
    ppermute x14, waiting for transfers between devices, per_device(): piece[PIECES - step] = lax.ppermute(near_r, 'fsdp', right)  76.4 us
    ppermute x14, starting transfers between devices, per_device(): piece[step] = lax.ppermute(near_l, 'fsdp', left)  69.7 us
    ppermute x14, starting transfers between devices, per_device(): piece[PIECES - step] = lax.ppermute(near_r, 'fsdp', right)  29.4 us
    all_to_all x1, blocking collectives, exchange(): lax.all_to_all(shaped, 'expert', split_axis=0, concat_axis=0, tiled=True)  29 us
    all_to_all x2, starting transfers between devices, exchange(): lax.all_to_all(shaped, 'expert', split_axis=0, concat_axis=0, tiled=True)  22.2 us
    pallas_call x2, Pallas kernels, expert_answers(): pl.pallas_call(functools.partial(expert_kernel, e), out_shape=jax.ShapeDt...  20.2 us
    ppermute x2, starting transfers between devices, per_device(): low = lax.ppermute(near_l[HALF:], 'fsdp', left)  9.13 us
  transfers between devices with their start and end apart: 34, of which 15 were waited for; matrix products, arithmetic and copies ran while one was open for 1% of the time, Pallas kernels for 9%

profile of v2, /device:TPU:1, one launch (start us, length us, event | category | flops | bytes accessed | tf_op | source)
XLA Modules:
  0.0 284.1 jit_solution(5044584278871833046)
XLA Ops:
  2.5 4.4 %collective-permute-start = (bf16[384,768]{1,0:T(8,128)(2,1)}, bf16[384,768]{1,0:T(8,128)(2,1)S(1)}, u32[]{:S(2)}, u32[]{:S(2)}) collective-permute-start(bf16[384,768]{1,0:T(8,128)(2,1)} %get-tuple-element.15.refs_0_), channel_id=1, source_target_pairs={{0,32},{32,64},{64,96},{96,128},{128,160},{160,192},{192,224},{224... | collective-permute-start | bytes 1769480 | tf_op jit(solution)/shard_map/ppermute | solution.py:367
  6.8 9.5 %collective-permute-start.3 = (bf16[384,768]{1,0:T(8,128)(2,1)}, bf16[384,768]{1,0:T(8,128)(2,1)S(1)}, u32[]{:S(2)}, u32[]{:S(2)}) collective-permute-start(bf16[384,768]{1,0:T(8,128)(2,1)} %get-tuple-element.15.refs_0_), channel_id=1, source_target_pairs={{0,480},{32,0},{64,32},{96,64},{128,96},{160,128},{192,160},{224,1... | collective-permute-start | bytes 1769480 | tf_op jit(solution)/shard_map/ppermute | solution.py:368
  16.3 11.3 %collective-permute-done.refs_14_ = bf16[384,768]{1,0:T(8,128)(2,1)S(1)} collective-permute-done((bf16[384,768]{1,0:T(8,128)(2,1)}, bf16[384,768]{1,0:T(8,128)(2,1)S(1)}, u32[]{:S(2)}, u32[]{:S(2)}) %collective-permute-start) | collective-permute-done | bytes 589856 | tf_op jit(solution)/shard_map/ppermute | solution.py:367
  30.4 4.6 %collective-permute-start.4 = (bf16[384,768]{1,0:T(8,128)(2,1)S(1)}, bf16[384,768]{1,0:T(8,128)(2,1)}, u32[]{:S(2)}, u32[]{:S(2)}) collective-permute-start(bf16[384,768]{1,0:T(8,128)(2,1)S(1)} %collective-permute-done.3.refs_1_), channel_id=1, source_target_pairs={{0,480},{32,0},{64,32},{96,64},{128,96},{160,128},{192,160},{224,1... | collective-permute-start | bytes 1769480 | tf_op jit(solution)/shard_map/ppermute | solution.py:368
  35.0 10.2 %collective-permute-done.1.refs_13_ = bf16[384,768]{1,0:T(8,128)(2,1)S(1)} collective-permute-done((bf16[384,768]{1,0:T(8,128)(2,1)S(1)}, bf16[384,768]{1,0:T(8,128)(2,1)S(1)}, u32[]{:S(2)}, u32[]{:S(2)}) %collective-permute-start.1) | collective-permute-done | bytes 589856 | tf_op jit(solution)/shard_map/ppermute | solution.py:367
  47.1 4.6 %collective-permute-start.5 = (bf16[384,768]{1,0:T(8,128)(2,1)}, bf16[384,768]{1,0:T(8,128)(2,1)}, u32[]{:S(2)}, u32[]{:S(2)}) collective-permute-start(bf16[384,768]{1,0:T(8,128)(2,1)} %collective-permute-done.4.refs_2_), channel_id=1, source_target_pairs={{0,480},{32,0},{64,32},{96,64},{128,96},{160,128},{192,160},{224,1... | collective-permute-start | bytes 1769480 | tf_op jit(solution)/shard_map/ppermute | solution.py:368
  53.6 4.6 %collective-permute-start.16 = (bf16[384,768]{1,0:T(8,128)(2,1)}, bf16[384,768]{1,0:T(8,128)(2,1)}, u32[]{:S(2)}, u32[]{:S(2)}) collective-permute-start(bf16[384,768]{1,0:T(8,128)(2,1)} %get-tuple-element.18.refs_0_), channel_id=1, source_target_pairs={{0,480},{32,0},{64,32},{96,64},{128,96},{160,128},{192,160},{224,1... | collective-permute-start | bytes 1769480 | tf_op jit(solution)/shard_map/ppermute | solution.py:368
  65.3 12.8 %all-to-all-start = ((bf16[32,16,2560]{2,1,0:T(8,128)(2,1)}), bf16[32,16,2560]{2,1,0:T(8,128)(2,1)S(1)}, u32[]{:S(2)}, u32[]{:S(2)}) async-start(bf16[32,16,2560]{2,1,0:T(8,128)(2,1)} %bitcast.23), calls=%async_computation | async-start | bytes 5242880 | tf_op jit(solution)/shard_map/all_to_all | solution.py:332
  80.1 4.6 %collective-permute-start.6 = (bf16[384,768]{1,0:T(8,128)(2,1)}, bf16[384,768]{1,0:T(8,128)(2,1)S(1)}, u32[]{:S(2)}, u32[]{:S(2)}) collective-permute-start(bf16[384,768]{1,0:T(8,128)(2,1)} %collective-permute-done.5.refs_3_), channel_id=1, source_target_pairs={{0,480},{32,0},{64,32},{96,64},{128,96},{160,128},{192,160},{224,1... | collective-permute-start | bytes 1769480 | tf_op jit(solution)/shard_map/ppermute | solution.py:368
  86.7 4.6 %collective-permute-start.17 = (bf16[384,768]{1,0:T(8,128)(2,1)}, bf16[384,768]{1,0:T(8,128)(2,1)S(1)}, u32[]{:S(2)}, u32[]{:S(2)}) collective-permute-start(bf16[384,768]{1,0:T(8,128)(2,1)} %collective-permute-done.16.refs_1_), channel_id=1, source_target_pairs={{0,480},{32,0},{64,32},{96,64},{128,96},{160,128},{192,160},{224,1... | collective-permute-start | bytes 1769480 | tf_op jit(solution)/shard_map/ppermute | solution.py:368
  91.2 5.0 %collective-permute-done.10.refs_11_ = bf16[384,768]{1,0:T(8,128)(2,1)S(1)} collective-permute-done((bf16[384,768]{1,0:T(8,128)(2,1)}, bf16[384,768]{1,0:T(8,128)(2,1)S(1)}, u32[]{:S(2)}, u32[]{:S(2)}) %collective-permute-start.10) | collective-permute-done | bytes 589856 | tf_op jit(solution)/shard_map/ppermute | solution.py:367
  98.1 4.6 %collective-permute-start.7 = (bf16[384,768]{1,0:T(8,128)(2,1)S(1)}, bf16[384,768]{1,0:T(8,128)(2,1)S(1)}, u32[]{:S(2)}, u32[]{:S(2)}) collective-permute-start(bf16[384,768]{1,0:T(8,128)(2,1)S(1)} %collective-permute-done.6.refs_4_), channel_id=1, source_target_pairs={{0,480},{32,0},{64,32},{96,64},{128,96},{160,128},{192,160},{224,1... | collective-permute-start | bytes 1769480 | tf_op jit(solution)/shard_map/ppermute | solution.py:368
  102.7 6.1 %collective-permute-done.24.refs_13_ = bf16[384,768]{1,0:T(8,128)(2,1)S(1)} collective-permute-done((bf16[384,768]{1,0:T(8,128)(2,1)}, bf16[384,768]{1,0:T(8,128)(2,1)S(1)}, u32[]{:S(2)}, u32[]{:S(2)}) %collective-permute-start.24) | collective-permute-done | bytes 589856 | tf_op jit(solution)/shard_map/ppermute | solution.py:367
  110.8 4.6 %collective-permute-start.18 = (bf16[384,768]{1,0:T(8,128)(2,1)S(1)}, bf16[384,768]{1,0:T(8,128)(2,1)S(1)}, u32[]{:S(2)}, u32[]{:S(2)}) collective-permute-start(bf16[384,768]{1,0:T(8,128)(2,1)S(1)} %collective-permute-done.17.refs_2_), channel_id=1, source_target_pairs={{0,480},{32,0},{64,32},{96,64},{128,96},{160,128},{192,160},{224,1... | collective-permute-start | bytes 1769480 | tf_op jit(solution)/shard_map/ppermute | solution.py:368
  115.4 6.1 %collective-permute-done.11.refs_10_ = bf16[384,768]{1,0:T(8,128)(2,1)S(1)} collective-permute-done((bf16[384,768]{1,0:T(8,128)(2,1)S(1)}, bf16[384,768]{1,0:T(8,128)(2,1)S(1)}, u32[]{:S(2)}, u32[]{:S(2)}) %collective-permute-start.11) | collective-permute-done | bytes 589856 | tf_op jit(solution)/shard_map/ppermute | solution.py:367
  123.4 4.6 %collective-permute-start.8 = (bf16[384,768]{1,0:T(8,128)(2,1)S(1)}, bf16[384,768]{1,0:T(8,128)(2,1)S(1)}, u32[]{:S(2)}, u32[]{:S(2)}) collective-permute-start(bf16[384,768]{1,0:T(8,128)(2,1)S(1)} %collective-permute-done.7.refs_5_), channel_id=1, source_target_pairs={{0,480},{32,0},{64,32},{96,64},{128,96},{160,128},{192,160},{224,1... | collective-permute-start | bytes 1769480 | tf_op jit(solution)/shard_map/ppermute | solution.py:368
  128.0 6.1 %collective-permute-done.25.refs_12_ = bf16[384,768]{1,0:T(8,128)(2,1)S(1)} collective-permute-done((bf16[384,768]{1,0:T(8,128)(2,1)S(1)}, bf16[384,768]{1,0:T(8,128)(2,1)S(1)}, u32[]{:S(2)}, u32[]{:S(2)}) %collective-permute-start.25) | collective-permute-done | bytes 589856 | tf_op jit(solution)/shard_map/ppermute | solution.py:367
  136.1 4.6 %collective-permute-start.19 = (bf16[384,768]{1,0:T(8,128)(2,1)S(1)}, bf16[384,768]{1,0:T(8,128)(2,1)}, u32[]{:S(2)}, u32[]{:S(2)}) collective-permute-start(bf16[384,768]{1,0:T(8,128)(2,1)S(1)} %collective-permute-done.18.refs_3_), channel_id=1, source_target_pairs={{0,480},{32,0},{64,32},{96,64},{128,96},{160,128},{192,160},{224,1... | collective-permute-start | bytes 1769480 | tf_op jit(solution)/shard_map/ppermute | solution.py:368
  140.6 6.1 %collective-permute-done.12.refs_9_ = bf16[384,768]{1,0:T(8,128)(2,1)S(1)} collective-permute-done((bf16[384,768]{1,0:T(8,128)(2,1)S(1)}, bf16[384,768]{1,0:T(8,128)(2,1)S(1)}, u32[]{:S(2)}, u32[]{:S(2)}) %collective-permute-start.12) | collective-permute-done | bytes 589856 | tf_op jit(solution)/shard_map/ppermute | solution.py:367
  148.7 4.6 %collective-permute-start.9 = (bf16[384,768]{1,0:T(8,128)(2,1)S(1)}, bf16[384,768]{1,0:T(8,128)(2,1)S(1)}, u32[]{:S(2)}, u32[]{:S(2)}) collective-permute-start(bf16[384,768]{1,0:T(8,128)(2,1)S(1)} %collective-permute-done.8.refs_6_), channel_id=1, source_target_pairs={{0,480},{32,0},{64,32},{96,64},{128,96},{160,128},{192,160},{224,1... | collective-permute-start | bytes 1769480 | tf_op jit(solution)/shard_map/ppermute | solution.py:368
  153.3 6.2 %collective-permute-done.26.refs_11_ = bf16[384,768]{1,0:T(8,128)(2,1)} collective-permute-done((bf16[384,768]{1,0:T(8,128)(2,1)S(1)}, bf16[384,768]{1,0:T(8,128)(2,1)}, u32[]{:S(2)}, u32[]{:S(2)}) %collective-permute-start.26) | collective-permute-done | bytes 589856 | tf_op jit(solution)/shard_map/ppermute | solution.py:367
  161.4 4.6 %collective-permute-start.20 = (bf16[384,768]{1,0:T(8,128)(2,1)}, bf16[384,768]{1,0:T(8,128)(2,1)}, u32[]{:S(2)}, u32[]{:S(2)}) collective-permute-start(bf16[384,768]{1,0:T(8,128)(2,1)} %collective-permute-done.19.refs_4_), channel_id=1, source_target_pairs={{0,480},{32,0},{64,32},{96,64},{128,96},{160,128},{192,160},{224,1... | collective-permute-start | bytes 1769480 | tf_op jit(solution)/shard_map/ppermute | solution.py:368
  166.1 5.9 %collective-permute-done.13.refs_8_ = bf16[384,768]{1,0:T(8,128)(2,1)S(1)} collective-permute-done((bf16[384,768]{1,0:T(8,128)(2,1)S(1)}, bf16[384,768]{1,0:T(8,128)(2,1)S(1)}, u32[]{:S(2)}, u32[]{:S(2)}) %collective-permute-start.13) | collective-permute-done | bytes 589856 | tf_op jit(solution)/shard_map/ppermute | solution.py:367
  174.9 4.6 %collective-permute-start.15 = (bf16[192,768]{1,0:T(8,128)(2,1)}, bf16[192,768]{1,0:T(8,128)(2,1)}, u32[]{:S(2)}, u32[]{:S(2)}) collective-permute-start(bf16[192,768]{1,0:T(8,128)(2,1)} %slice.17), channel_id=1, source_target_pairs={{0,480},{32,0},{64,32},{96,64},{128,96},{160,128},{192,160},{224,1... | collective-permute-start | bytes 884744 | tf_op jit(solution)/shard_map/ppermute | solution.py:371
  186.7 4.6 %collective-permute-start.21 = (bf16[384,768]{1,0:T(8,128)(2,1)}, bf16[384,768]{1,0:T(8,128)(2,1)S(1)}, u32[]{:S(2)}, u32[]{:S(2)}) collective-permute-start(bf16[384,768]{1,0:T(8,128)(2,1)} %collective-permute-done.20.refs_5_), channel_id=1, source_target_pairs={{0,480},{32,0},{64,32},{96,64},{128,96},{160,128},{192,160},{224,1... | collective-permute-start | bytes 1769480 | tf_op jit(solution)/shard_map/ppermute | solution.py:368
  192.0 10.1 %shard_map.103 = bf16[256,2560]{1,0:T(8,128)(2,1)} custom-call(s32[1]{0:T(128)} %bitcast.me, bf16[2,320,2048]{2,1,0:T(8,128)(2,1)} %copy-done, bf16[384,768]{1,0:T(8,128)(2,1)} %get-tuple-element.15.refs_0_, bf16[384,768]{1,0:T(8,128)(2,1)} %copy-done.10, bf16[384,768]{1,0:T(8,128)(2,1)} %collective-permute-done.4.refs_2_, ...), custom_call_target="tpu_custom_call" | custom-call | flops 3019898880 | bytes 13631488 | tf_op jit(solution)/shard_map/pallas_call | solution.py:301
  202.1 9.3 %all-to-all-start.1 = ((bf16[32,8,2560]{2,1,0:T(8,128)(2,1)}), bf16[32,8,2560]{2,1,0:T(8,128)(2,1)S(1)}, u32[]{:S(2)}, u32[]{:S(2)}) async-start(bf16[32,8,2560]{2,1,0:T(8,128)(2,1)} %bitcast.29), calls=%async_computation.1 | async-start | bytes 2621440 | tf_op jit(solution)/shard_map/all_to_all | solution.py:332
  213.5 5.3 %collective-permute-start.22 = (bf16[384,768]{1,0:T(8,128)(2,1)S(1)}, bf16[384,768]{1,0:T(8,128)(2,1)S(1)}, u32[]{:S(2)}, u32[]{:S(2)}) collective-permute-start(bf16[384,768]{1,0:T(8,128)(2,1)S(1)} %collective-permute-done.21.refs_6_), channel_id=1, source_target_pairs={{0,480},{32,0},{64,32},{96,64},{128,96},{160,128},{192,160},{224,1... | collective-permute-start | bytes 1769480 | tf_op jit(solution)/shard_map/ppermute | solution.py:368
  218.9 11.4 %collective-permute-done.29.refs_8_ = bf16[384,768]{1,0:T(8,128)(2,1)S(1)} collective-permute-done((bf16[384,768]{1,0:T(8,128)(2,1)S(1)}, bf16[384,768]{1,0:T(8,128)(2,1)S(1)}, u32[]{:S(2)}, u32[]{:S(2)}) %collective-permute-start.29) | collective-permute-done | bytes 589856 | tf_op jit(solution)/shard_map/ppermute | solution.py:367
  232.3 4.6 %collective-permute-start.31 = (bf16[192,768]{1,0:T(8,128)(2,1)S(1)}, bf16[192,768]{1,0:T(8,128)(2,1)S(1)}, u32[]{:S(2)}, u32[]{:S(2)}) collective-permute-start(bf16[192,768]{1,0:T(8,128)(2,1)S(1)} %slice.19), channel_id=1, source_target_pairs={{0,480},{32,0},{64,32},{96,64},{128,96},{160,128},{192,160},{224,1... | collective-permute-start | bytes 884744 | tf_op jit(solution)/shard_map/ppermute | solution.py:371
  242.9 10.1 %shard_map.104 = bf16[256,2560]{1,0:T(8,128)(2,1)} custom-call(s32[1]{0:T(128)} %bitcast.me, bf16[2,320,2048]{2,1,0:T(8,128)(2,1)} %copy-done, bf16[384,768]{1,0:T(8,128)(2,1)} %get-tuple-element.18.refs_0_, bf16[384,768]{1,0:T(8,128)(2,1)} %collective-permute-done.16.refs_1_, bf16[384,768]{1,0:T(8,128)(2,1)} %copy-done.14, bf16[384,768]{1,0:T(8,128)(2,1)} %copy-done.16, ...), custom_call_target="tpu_custom_call" | custom-call | flops 3019898880 | bytes 13631488 | tf_op jit(solution)/shard_map/pallas_call | solution.py:301
  253.0 29.0 %all_to_all.15 = bf16[32,8,2560]{2,1,0:T(8,128)(2,1)S(1)} all-to-all(bf16[32,8,2560]{2,1,0:T(8,128)(2,1)} %bitcast.30), channel_id=1, replica_groups=mesh['fsdp'=16,'expert'=32] {'expert'}, dimensions={0} | all-to-all | bytes 2621440 | tf_op jit(solution)/shard_map/all_to_all | solution.py:332
  (116 shorter events, 54.3 us)
Async XLA Ops:
  2.5 25.2 %collective-permute-start = (bf16[384,768]{1,0:T(8,128)(2,1)}, bf16[384,768]{1,0:T(8,128)(2,1)S(1)}, u32[]{:S(2)}, u32[]{:S(2)}) collective-permute-start(bf16[384,768]{1,0:T(8,128)(2,1)} %get-tuple-element.15.refs_0_), channel_id=1, source_target_pairs={{0,32},{32,64},{64,96},{96,128},{128,160},{160,192},{192,224},{224... | collective-permute-start | bytes 1769480 | tf_op jit(solution)/shard_map/ppermute | solution.py:367
  6.8 23.6 %collective-permute-start.3 = (bf16[384,768]{1,0:T(8,128)(2,1)}, bf16[384,768]{1,0:T(8,128)(2,1)S(1)}, u32[]{:S(2)}, u32[]{:S(2)}) collective-permute-start(bf16[384,768]{1,0:T(8,128)(2,1)} %get-tuple-element.15.refs_0_), channel_id=1, source_target_pairs={{0,480},{32,0},{64,32},{96,64},{128,96},{160,128},{192,160},{224,1... | collective-permute-start | bytes 1769480 | tf_op jit(solution)/shard_map/ppermute | solution.py:368
  28.5 16.7 %collective-permute-start.1 = (bf16[384,768]{1,0:T(8,128)(2,1)S(1)}, bf16[384,768]{1,0:T(8,128)(2,1)S(1)}, u32[]{:S(2)}, u32[]{:S(2)}) collective-permute-start(bf16[384,768]{1,0:T(8,128)(2,1)S(1)} %collective-permute-done.refs_14_), channel_id=1, source_target_pairs={{0,32},{32,64},{64,96},{96,128},{128,160},{160,192},{192,224},{224... | collective-permute-start | bytes 1769480 | tf_op jit(solution)/shard_map/ppermute | solution.py:367
  30.4 16.7 %collective-permute-start.4 = (bf16[384,768]{1,0:T(8,128)(2,1)S(1)}, bf16[384,768]{1,0:T(8,128)(2,1)}, u32[]{:S(2)}, u32[]{:S(2)}) collective-permute-start(bf16[384,768]{1,0:T(8,128)(2,1)S(1)} %collective-permute-done.3.refs_1_), channel_id=1, source_target_pairs={{0,480},{32,0},{64,32},{96,64},{128,96},{160,128},{192,160},{224,1... | collective-permute-start | bytes 1769480 | tf_op jit(solution)/shard_map/ppermute | solution.py:368
  45.2 15.8 %collective-permute-start.2 = (bf16[384,768]{1,0:T(8,128)(2,1)S(1)}, bf16[384,768]{1,0:T(8,128)(2,1)S(1)}, u32[]{:S(2)}, u32[]{:S(2)}) collective-permute-start(bf16[384,768]{1,0:T(8,128)(2,1)S(1)} %collective-permute-done.1.refs_13_), channel_id=1, source_target_pairs={{0,32},{32,64},{64,96},{96,128},{128,160},{160,192},{192,224},{224... | collective-permute-start | bytes 1769480 | tf_op jit(solution)/shard_map/ppermute | solution.py:367
  47.1 33.0 %collective-permute-start.5 = (bf16[384,768]{1,0:T(8,128)(2,1)}, bf16[384,768]{1,0:T(8,128)(2,1)}, u32[]{:S(2)}, u32[]{:S(2)}) collective-permute-start(bf16[384,768]{1,0:T(8,128)(2,1)} %collective-permute-done.4.refs_2_), channel_id=1, source_target_pairs={{0,480},{32,0},{64,32},{96,64},{128,96},{160,128},{192,160},{224,1... | collective-permute-start | bytes 1769480 | tf_op jit(solution)/shard_map/ppermute | solution.py:368
  51.7 33.0 %collective-permute-start.23 = (bf16[384,768]{1,0:T(8,128)(2,1)}, bf16[384,768]{1,0:T(8,128)(2,1)}, u32[]{:S(2)}, u32[]{:S(2)}) collective-permute-start(bf16[384,768]{1,0:T(8,128)(2,1)} %get-tuple-element.18.refs_0_), channel_id=1, source_target_pairs={{0,32},{32,64},{64,96},{96,128},{128,160},{160,192},{192,224},{224... | collective-permute-start | bytes 1769480 | tf_op jit(solution)/shard_map/ppermute | solution.py:367
  53.6 33.0 %collective-permute-start.16 = (bf16[384,768]{1,0:T(8,128)(2,1)}, bf16[384,768]{1,0:T(8,128)(2,1)}, u32[]{:S(2)}, u32[]{:S(2)}) collective-permute-start(bf16[384,768]{1,0:T(8,128)(2,1)} %get-tuple-element.18.refs_0_), channel_id=1, source_target_pairs={{0,480},{32,0},{64,32},{96,64},{128,96},{160,128},{192,160},{224,1... | collective-permute-start | bytes 1769480 | tf_op jit(solution)/shard_map/ppermute | solution.py:368
  65.3 114.2 %all-to-all-start = ((bf16[32,16,2560]{2,1,0:T(8,128)(2,1)}), bf16[32,16,2560]{2,1,0:T(8,128)(2,1)S(1)}, u32[]{:S(2)}, u32[]{:S(2)}) async-start(bf16[32,16,2560]{2,1,0:T(8,128)(2,1)} %bitcast.23), calls=%async_computation | async-start | bytes 5242880 | tf_op jit(solution)/shard_map/all_to_all | solution.py:332
  78.2 18.0 %collective-permute-start.10 = (bf16[384,768]{1,0:T(8,128)(2,1)}, bf16[384,768]{1,0:T(8,128)(2,1)S(1)}, u32[]{:S(2)}, u32[]{:S(2)}) collective-permute-start(bf16[384,768]{1,0:T(8,128)(2,1)} %copy-done.12), channel_id=1, source_target_pairs={{0,32},{32,64},{64,96},{96,128},{128,160},{160,192},{192,224},{224... | collective-permute-start | bytes 1769480 | tf_op jit(solution)/shard_map/ppermute | solution.py:367
  80.1 18.0 %collective-permute-start.6 = (bf16[384,768]{1,0:T(8,128)(2,1)}, bf16[384,768]{1,0:T(8,128)(2,1)S(1)}, u32[]{:S(2)}, u32[]{:S(2)}) collective-permute-start(bf16[384,768]{1,0:T(8,128)(2,1)} %collective-permute-done.5.refs_3_), channel_id=1, source_target_pairs={{0,480},{32,0},{64,32},{96,64},{128,96},{160,128},{192,160},{224,1... | collective-permute-start | bytes 1769480 | tf_op jit(solution)/shard_map/ppermute | solution.py:368
  84.7 24.1 %collective-permute-start.24 = (bf16[384,768]{1,0:T(8,128)(2,1)}, bf16[384,768]{1,0:T(8,128)(2,1)S(1)}, u32[]{:S(2)}, u32[]{:S(2)}) collective-permute-start(bf16[384,768]{1,0:T(8,128)(2,1)} %collective-permute-done.23.refs_14_), channel_id=1, source_target_pairs={{0,32},{32,64},{64,96},{96,128},{128,160},{160,192},{192,224},{224... | collective-permute-start | bytes 1769480 | tf_op jit(solution)/shard_map/ppermute | solution.py:367
  86.7 24.1 %collective-permute-start.17 = (bf16[384,768]{1,0:T(8,128)(2,1)}, bf16[384,768]{1,0:T(8,128)(2,1)S(1)}, u32[]{:S(2)}, u32[]{:S(2)}) collective-permute-start(bf16[384,768]{1,0:T(8,128)(2,1)} %collective-permute-done.16.refs_1_), channel_id=1, source_target_pairs={{0,480},{32,0},{64,32},{96,64},{128,96},{160,128},{192,160},{224,1... | collective-permute-start | bytes 1769480 | tf_op jit(solution)/shard_map/ppermute | solution.py:368
  96.2 25.3 %collective-permute-start.11 = (bf16[384,768]{1,0:T(8,128)(2,1)S(1)}, bf16[384,768]{1,0:T(8,128)(2,1)S(1)}, u32[]{:S(2)}, u32[]{:S(2)}) collective-permute-start(bf16[384,768]{1,0:T(8,128)(2,1)S(1)} %collective-permute-done.10.refs_11_), channel_id=1, source_target_pairs={{0,32},{32,64},{64,96},{96,128},{128,160},{160,192},{192,224},{224... | collective-permute-start | bytes 1769480 | tf_op jit(solution)/shard_map/ppermute | solution.py:367
  98.1 25.3 %collective-permute-start.7 = (bf16[384,768]{1,0:T(8,128)(2,1)S(1)}, bf16[384,768]{1,0:T(8,128)(2,1)S(1)}, u32[]{:S(2)}, u32[]{:S(2)}) collective-permute-start(bf16[384,768]{1,0:T(8,128)(2,1)S(1)} %collective-permute-done.6.refs_4_), channel_id=1, source_target_pairs={{0,480},{32,0},{64,32},{96,64},{128,96},{160,128},{192,160},{224,1... | collective-permute-start | bytes 1769480 | tf_op jit(solution)/shard_map/ppermute | solution.py:368
  108.8 25.3 %collective-permute-start.25 = (bf16[384,768]{1,0:T(8,128)(2,1)S(1)}, bf16[384,768]{1,0:T(8,128)(2,1)S(1)}, u32[]{:S(2)}, u32[]{:S(2)}) collective-permute-start(bf16[384,768]{1,0:T(8,128)(2,1)S(1)} %collective-permute-done.24.refs_13_), channel_id=1, source_target_pairs={{0,32},{32,64},{64,96},{96,128},{128,160},{160,192},{192,224},{224... | collective-permute-start | bytes 1769480 | tf_op jit(solution)/shard_map/ppermute | solution.py:367
  110.8 25.3 %collective-permute-start.18 = (bf16[384,768]{1,0:T(8,128)(2,1)S(1)}, bf16[384,768]{1,0:T(8,128)(2,1)S(1)}, u32[]{:S(2)}, u32[]{:S(2)}) collective-permute-start(bf16[384,768]{1,0:T(8,128)(2,1)S(1)} %collective-permute-done.17.refs_2_), channel_id=1, source_target_pairs={{0,480},{32,0},{64,32},{96,64},{128,96},{160,128},{192,160},{224,1... | collective-permute-start | bytes 1769480 | tf_op jit(solution)/shard_map/ppermute | solution.py:368
  121.5 25.3 %collective-permute-start.12 = (bf16[384,768]{1,0:T(8,128)(2,1)S(1)}, bf16[384,768]{1,0:T(8,128)(2,1)S(1)}, u32[]{:S(2)}, u32[]{:S(2)}) collective-permute-start(bf16[384,768]{1,0:T(8,128)(2,1)S(1)} %collective-permute-done.11.refs_10_), channel_id=1, source_target_pairs={{0,32},{32,64},{64,96},{96,128},{128,160},{160,192},{192,224},{224... | collective-permute-start | bytes 1769480 | tf_op jit(solution)/shard_map/ppermute | solution.py:367
  123.4 25.3 %collective-permute-start.8 = (bf16[384,768]{1,0:T(8,128)(2,1)S(1)}, bf16[384,768]{1,0:T(8,128)(2,1)S(1)}, u32[]{:S(2)}, u32[]{:S(2)}) collective-permute-start(bf16[384,768]{1,0:T(8,128)(2,1)S(1)} %collective-permute-done.7.refs_5_), channel_id=1, source_target_pairs={{0,480},{32,0},{64,32},{96,64},{128,96},{160,128},{192,160},{224,1... | collective-permute-start | bytes 1769480 | tf_op jit(solution)/shard_map/ppermute | solution.py:368
  134.1 25.4 %collective-permute-start.26 = (bf16[384,768]{1,0:T(8,128)(2,1)S(1)}, bf16[384,768]{1,0:T(8,128)(2,1)}, u32[]{:S(2)}, u32[]{:S(2)}) collective-permute-start(bf16[384,768]{1,0:T(8,128)(2,1)S(1)} %collective-permute-done.25.refs_12_), channel_id=1, source_target_pairs={{0,32},{32,64},{64,96},{96,128},{128,160},{160,192},{192,224},{224... | collective-permute-start | bytes 1769480 | tf_op jit(solution)/shard_map/ppermute | solution.py:367
  136.1 25.4 %collective-permute-start.19 = (bf16[384,768]{1,0:T(8,128)(2,1)S(1)}, bf16[384,768]{1,0:T(8,128)(2,1)}, u32[]{:S(2)}, u32[]{:S(2)}) collective-permute-start(bf16[384,768]{1,0:T(8,128)(2,1)S(1)} %collective-permute-done.18.refs_3_), channel_id=1, source_target_pairs={{0,480},{32,0},{64,32},{96,64},{128,96},{160,128},{192,160},{224,1... | collective-permute-start | bytes 1769480 | tf_op jit(solution)/shard_map/ppermute | solution.py:368
  146.8 25.3 %collective-permute-start.13 = (bf16[384,768]{1,0:T(8,128)(2,1)S(1)}, bf16[384,768]{1,0:T(8,128)(2,1)S(1)}, u32[]{:S(2)}, u32[]{:S(2)}) collective-permute-start(bf16[384,768]{1,0:T(8,128)(2,1)S(1)} %collective-permute-done.12.refs_9_), channel_id=1, source_target_pairs={{0,32},{32,64},{64,96},{96,128},{128,160},{160,192},{192,224},{224... | collective-permute-start | bytes 1769480 | tf_op jit(solution)/shard_map/ppermute | solution.py:367
  148.7 25.3 %collective-permute-start.9 = (bf16[384,768]{1,0:T(8,128)(2,1)S(1)}, bf16[384,768]{1,0:T(8,128)(2,1)S(1)}, u32[]{:S(2)}, u32[]{:S(2)}) collective-permute-start(bf16[384,768]{1,0:T(8,128)(2,1)S(1)} %collective-permute-done.8.refs_6_), channel_id=1, source_target_pairs={{0,480},{32,0},{64,32},{96,64},{128,96},{160,128},{192,160},{224,1... | collective-permute-start | bytes 1769480 | tf_op jit(solution)/shard_map/ppermute | solution.py:368
  159.5 25.3 %collective-permute-start.27 = (bf16[384,768]{1,0:T(8,128)(2,1)}, bf16[384,768]{1,0:T(8,128)(2,1)}, u32[]{:S(2)}, u32[]{:S(2)}) collective-permute-start(bf16[384,768]{1,0:T(8,128)(2,1)} %collective-permute-done.26.refs_11_), channel_id=1, source_target_pairs={{0,32},{32,64},{64,96},{96,128},{128,160},{160,192},{192,224},{224... | collective-permute-start | bytes 1769480 | tf_op jit(solution)/shard_map/ppermute | solution.py:367
  161.4 25.3 %collective-permute-start.20 = (bf16[384,768]{1,0:T(8,128)(2,1)}, bf16[384,768]{1,0:T(8,128)(2,1)}, u32[]{:S(2)}, u32[]{:S(2)}) collective-permute-start(bf16[384,768]{1,0:T(8,128)(2,1)} %collective-permute-done.19.refs_4_), channel_id=1, source_target_pairs={{0,480},{32,0},{64,32},{96,64},{128,96},{160,128},{192,160},{224,1... | collective-permute-start | bytes 1769480 | tf_op jit(solution)/shard_map/ppermute | solution.py:368
  172.1 19.2 %collective-permute-start.14 = (bf16[192,768]{1,0:T(8,128)(2,1)S(1)}, bf16[192,768]{1,0:T(8,128)(2,1)}, u32[]{:S(2)}, u32[]{:S(2)}) collective-permute-start(bf16[192,768]{1,0:T(8,128)(2,1)S(1)} %slice.16), channel_id=1, source_target_pairs={{0,32},{32,64},{64,96},{96,128},{128,160},{160,192},{192,224},{224... | collective-permute-start | bytes 884744 | tf_op jit(solution)/shard_map/ppermute | solution.py:370
  174.9 17.0 %collective-permute-start.15 = (bf16[192,768]{1,0:T(8,128)(2,1)}, bf16[192,768]{1,0:T(8,128)(2,1)}, u32[]{:S(2)}, u32[]{:S(2)}) collective-permute-start(bf16[192,768]{1,0:T(8,128)(2,1)} %slice.17), channel_id=1, source_target_pairs={{0,480},{32,0},{64,32},{96,64},{128,96},{160,128},{192,160},{224,1... | collective-permute-start | bytes 884744 | tf_op jit(solution)/shard_map/ppermute | solution.py:371
  184.8 26.6 %collective-permute-start.28 = (bf16[384,768]{1,0:T(8,128)(2,1)}, bf16[384,768]{1,0:T(8,128)(2,1)S(1)}, u32[]{:S(2)}, u32[]{:S(2)}) collective-permute-start(bf16[384,768]{1,0:T(8,128)(2,1)} %collective-permute-done.27.refs_10_), channel_id=1, source_target_pairs={{0,32},{32,64},{64,96},{96,128},{128,160},{160,192},{192,224},{224... | collective-permute-start | bytes 1769480 | tf_op jit(solution)/shard_map/ppermute | solution.py:367
  186.7 26.8 %collective-permute-start.21 = (bf16[384,768]{1,0:T(8,128)(2,1)}, bf16[384,768]{1,0:T(8,128)(2,1)S(1)}, u32[]{:S(2)}, u32[]{:S(2)}) collective-permute-start(bf16[384,768]{1,0:T(8,128)(2,1)} %collective-permute-done.20.refs_5_), channel_id=1, source_target_pairs={{0,480},{32,0},{64,32},{96,64},{128,96},{160,128},{192,160},{224,1... | collective-permute-start | bytes 1769480 | tf_op jit(solution)/shard_map/ppermute | solution.py:368
  202.1 50.9 %all-to-all-start.1 = ((bf16[32,8,2560]{2,1,0:T(8,128)(2,1)}), bf16[32,8,2560]{2,1,0:T(8,128)(2,1)S(1)}, u32[]{:S(2)}, u32[]{:S(2)}) async-start(bf16[32,8,2560]{2,1,0:T(8,128)(2,1)} %bitcast.29), calls=%async_computation.1 | async-start | bytes 2621440 | tf_op jit(solution)/shard_map/all_to_all | solution.py:332
  211.4 18.9 %collective-permute-start.29 = (bf16[384,768]{1,0:T(8,128)(2,1)S(1)}, bf16[384,768]{1,0:T(8,128)(2,1)S(1)}, u32[]{:S(2)}, u32[]{:S(2)}) collective-permute-start(bf16[384,768]{1,0:T(8,128)(2,1)S(1)} %collective-permute-done.28.refs_9_), channel_id=1, source_target_pairs={{0,32},{32,64},{64,96},{96,128},{128,160},{160,192},{192,224},{224... | collective-permute-start | bytes 1769480 | tf_op jit(solution)/shard_map/ppermute | solution.py:367
  213.5 18.7 %collective-permute-start.22 = (bf16[384,768]{1,0:T(8,128)(2,1)S(1)}, bf16[384,768]{1,0:T(8,128)(2,1)S(1)}, u32[]{:S(2)}, u32[]{:S(2)}) collective-permute-start(bf16[384,768]{1,0:T(8,128)(2,1)S(1)} %collective-permute-done.21.refs_6_), channel_id=1, source_target_pairs={{0,480},{32,0},{64,32},{96,64},{128,96},{160,128},{192,160},{224,1... | collective-permute-start | bytes 1769480 | tf_op jit(solution)/shard_map/ppermute | solution.py:368
  (32 other events, 953.7 us)

commit v3 on v1

--- a/solution.py
+++ b/solution.py
@@ -9,6 +9,7 @@
 GROUP = 2
 LANE = 128
 VMEM_LIMIT = 56 * 1024 * 1024
+SMALL_LIMIT = 24 * 1024 * 1024
 
 TOK = 128
 CHOICES = TOK * TOP
@@ -24,6 +25,8 @@
 PIECES = 16
 PIECE = 3 * LANE
 HALF = PIECE // 2
+KSTEP = 2
+GATE = 0
 
 
 def iota(shape, axis):
@@ -246,8 +249,8 @@
     out[...] = (before[...] + mix(0, ans, s_hi, s_lo, p_hi, p_lo)).astype(jnp.bfloat16)
 
 
-def params():
-    return pltpu.CompilerParams(vmem_limit_bytes=VMEM_LIMIT)
+def params(size=SMALL_LIMIT):
+    return pltpu.CompilerParams(vmem_limit_bytes=size)
 
 
 def vmem(count):
@@ -291,7 +294,7 @@
         out_shape=[jax.ShapeDtypeStruct((PIECE, HID), jnp.bfloat16), half, half],
         in_specs=vmem(3),
         out_specs=vmem(3),
-        compiler_params=params(),
+        compiler_params=params(VMEM_LIMIT),
         cost_estimate=cost(0, 8 * PIECE * HID),
     )(gate_weight, up_weight, down_weight)
 
@@ -327,7 +330,7 @@
             pltpu.SemaphoreType.DMA((3, 4)),
             pltpu.SemaphoreType.DMA,
         ],
-        compiler_params=params(),
+        compiler_params=params(VMEM_LIMIT),
         cost_estimate=EXPERT_COST,
     )(x, weights)
 
@@ -339,7 +342,7 @@
         in_specs=[SMEM] + vmem(1) + anywhere(len(pieces)),
         out_specs=vmem(1)[0],
         scratch_shapes=[*expert_scratch(), pltpu.SemaphoreType.DMA((4, PIECES))],
-        compiler_params=params(),
+        compiler_params=params(VMEM_LIMIT),
         cost_estimate=EXPERT_COST,
     )(me, x, *pieces)
 
@@ -385,22 +388,27 @@
     left = [(i, (i - 1) % PIECES) for i in range(PIECES)]
 
     own, high, low = pack(gate_weight, up_weight, down_weight)
-    weights = lax.all_gather(own, "fsdp")
     highs, lows = {0: high}, {0: low}
     half = PIECES // 2
     for step in range(1, half + 1):
-        highs[PIECES - step] = lax.ppermute(highs[(PIECES - step + 1) % PIECES], "fsdp", right)
-        lows[step] = lax.ppermute(lows[step - 1], "fsdp", left)
+        near_r, near_l = highs[(PIECES - step + 1) % PIECES], lows[step - 1]
+        if step == GATE + 1:
+            weights = lax.all_gather(after(own, near_r) if GATE else own, "fsdp")
+        if step == KSTEP + 1:
+            ready = after(tokens, near_r, near_l, highs[step - 1], lows[PIECES - step + 1])
+            out, *scales = dispatch(expert_ids, priority, overflow_pick, partner, capacity, route_scale, ready)
+            x = split_rows(exchange(out))
+        highs[PIECES - step] = lax.ppermute(near_r, "fsdp", right)
+        lows[step] = lax.ppermute(near_l, "fsdp", left)
         if step < half:
             highs[step] = lax.ppermute(highs[step - 1], "fsdp", left)
             lows[PIECES - step] = lax.ppermute(lows[(PIECES - step + 1) % PIECES], "fsdp", right)
     pieces = [highs[j] for j in range(PIECES)] + [lows[j] for j in range(PIECES)]
 
-    ready = after(tokens, highs[PIECES - 1], lows[1])
-    out, *scales = dispatch(expert_ids, priority, overflow_pick, partner, capacity, route_scale, ready)
-    x = split_rows(exchange(out))
     second = second_expert(me, x, pieces)
-    first = first_expert(after(x, second), weights)
+    far = PIECES // 2 - 1
+    x0 = after(x, highs[PIECES - far], lows[far])
+    first = first_expert(x0, weights)
     before = combine(exchange(second), scales)
     return combine_last(exchange(first), scales, before)
 

time: 293 us -> 288 us (0.983)
  Pallas kernels: 38.5 us -> 27.8 us
  starting transfers between devices: 124 us -> 132 us
  waiting for transfers between devices: 105 us -> 100 us
    ppermute x7, waiting for transfers between devices: 0.02 us -> 45.1 us  [per_device(): highs[step] = lax.ppermute(highs[step - 1], 'fsdp', left)]
    ppermute x7, waiting for transfers between devices: 35.8 us -> 0.02 us  [per_device(): lax.ppermute(lows[(PIECES - step + 1) % PIECES], 'fsdp', right)]
    ppermute x16, waiting for transfers between devices: 40.4 us -> 25 us  [the longest x8 24.9 us: per_device(): highs[PIECES - step] = lax.ppermute(near_r, 'fsdp', right)]
    all_to_all x3, starting transfers between devices: 19.6 us -> 25.4 us  [exchange(): lax.all_to_all(shaped, 'expert', split_axis=0, concat_axis=0, tiled=True)]
    unnamed x58 -> x60, local copies, waits for them, and re-layouts: 4.62 us -> 9.08 us
    pallas_call x1, Pallas kernels: 5.29 us -> 2.03 us  [split_rows(): pl.pallas_call(split_kernel, out_shape=jax.ShapeDtypeStruct((2, ROWS_E, D...]
    pallas_call x1, Pallas kernels: 5.94 us -> 2.86 us  [dispatch(): pl.pallas_call(dispatch_kernel, out_shape=[jax.ShapeDtypeStruct((MAIN, D...]
  transfers between devices with their start and end apart: 34 -> 34, of which waited for: 15 -> 15; matrix products, arithmetic and copies ran while one was open for 3% -> 2% of each run, Pallas kernels for 11% -> 8%
where the time goes in v3:
time: 288 us; the launch traced here: 287 us
  starting transfers between devices  132 us (46%)
  waiting for transfers between devices  100 us (35%)
  Pallas kernels  27.8 us (10%)
  between operations  14 us (5%)
  local copies, waits for them, and re-layouts  10.9 us (4%)
    ppermute x7, waiting for transfers between devices, per_device(): highs[step] = lax.ppermute(highs[step - 1], 'fsdp', left)  45.1 us
    ppermute x8, starting transfers between devices, per_device(): lows[step] = lax.ppermute(near_l, 'fsdp', left)  42 us
    ppermute x7, starting transfers between devices, per_device(): highs[step] = lax.ppermute(highs[step - 1], 'fsdp', left)  33.2 us
    all_to_all x3, waiting for transfers between devices, exchange(): lax.all_to_all(shaped, 'expert', split_axis=0, concat_axis=0, tiled=True)  29.9 us
    all_to_all x3, starting transfers between devices, exchange(): lax.all_to_all(shaped, 'expert', split_axis=0, concat_axis=0, tiled=True)  25.4 us
    ppermute x8, waiting for transfers between devices, per_device(): highs[PIECES - step] = lax.ppermute(near_r, 'fsdp', right)  24.9 us
    ppermute x8, starting transfers between devices, per_device(): highs[PIECES - step] = lax.ppermute(near_r, 'fsdp', right)  17.8 us
    ppermute x7, starting transfers between devices, per_device(): lax.ppermute(lows[(PIECES - step + 1) % PIECES], 'fsdp', right)  13.8 us
  transfers between devices with their start and end apart: 34, of which 15 were waited for; matrix products, arithmetic and copies ran while one was open for 2% of the time, Pallas kernels for 8%

profile of v3, /device:TPU:1, one launch (start us, length us, event | category | flops | bytes accessed | tf_op | source)
XLA Modules:
  0.0 286.9 jit_solution(12308963140153100999)
XLA Ops:
  8.9 4.4 %collective-permute-start = (bf16[192,768]{1,0:T(8,128)(2,1)}, bf16[192,768]{1,0:T(8,128)(2,1)S(1)}, u32[]{:S(2)}, u32[]{:S(2)}) collective-permute-start(bf16[192,768]{1,0:T(8,128)(2,1)} %get-tuple-element.15.refs_0_), channel_id=1, source_target_pairs={{0,32},{32,64},{64,96},{96,128},{128,160},{160,192},{192,224},{224... | collective-permute-start | bytes 884744 | tf_op jit(solution)/shard_map/ppermute | solution.py:401
  13.3 9.5 %collective-permute-start.2 = (bf16[192,768]{1,0:T(8,128)(2,1)}, bf16[192,768]{1,0:T(8,128)(2,1)S(1)}, u32[]{:S(2)}, u32[]{:S(2)}) collective-permute-start(bf16[192,768]{1,0:T(8,128)(2,1)} %get-tuple-element.16.refs_16_), channel_id=1, source_target_pairs={{0,480},{32,0},{64,32},{96,64},{128,96},{160,128},{192,160},{224,1... | collective-permute-start | bytes 884744 | tf_op jit(solution)/shard_map/ppermute | solution.py:402
  30.0 4.6 %collective-permute-start.3 = (bf16[192,768]{1,0:T(8,128)(2,1)S(1)}, bf16[192,768]{1,0:T(8,128)(2,1)S(1)}, u32[]{:S(2)}, u32[]{:S(2)}) collective-permute-start(bf16[192,768]{1,0:T(8,128)(2,1)S(1)} %collective-permute-done.2.refs_17_), channel_id=1, source_target_pairs={{0,480},{32,0},{64,32},{96,64},{128,96},{160,128},{192,160},{224,1... | collective-permute-start | bytes 884744 | tf_op jit(solution)/shard_map/ppermute | solution.py:402
  34.6 3.7 %collective-permute-done.4.refs_1_ = bf16[192,768]{1,0:T(8,128)(2,1)S(1)} collective-permute-done((bf16[192,768]{1,0:T(8,128)(2,1)}, bf16[192,768]{1,0:T(8,128)(2,1)S(1)}, u32[]{:S(2)}, u32[]{:S(2)}) %collective-permute-start.4) | collective-permute-done | bytes 294944 | tf_op jit(solution)/shard_map/ppermute | solution.py:404
  38.4 5.3 %collective-permute-start.5 = (bf16[192,768]{1,0:T(8,128)(2,1)S(1)}, bf16[192,768]{1,0:T(8,128)(2,1)S(1)}, u32[]{:S(2)}, u32[]{:S(2)}) collective-permute-start(bf16[192,768]{1,0:T(8,128)(2,1)S(1)} %collective-permute-done.4.refs_1_), channel_id=1, source_target_pairs={{0,480},{32,0},{64,32},{96,64},{128,96},{160,128},{192,160},{224,1... | collective-permute-start | bytes 884744 | tf_op jit(solution)/shard_map/ppermute | solution.py:404
  50.9 12.6 %collective-permute-done.5.refs_2_ = bf16[192,768]{1,0:T(8,128)(2,1)S(1)} collective-permute-done((bf16[192,768]{1,0:T(8,128)(2,1)S(1)}, bf16[192,768]{1,0:T(8,128)(2,1)S(1)}, u32[]{:S(2)}, u32[]{:S(2)}) %collective-permute-start.5) | collective-permute-done | bytes 294944 | tf_op jit(solution)/shard_map/ppermute | solution.py:404
  70.4 12.6 %all-to-all-start = ((bf16[32,16,2560]{2,1,0:T(8,128)(2,1)}), bf16[32,16,2560]{2,1,0:T(8,128)(2,1)S(1)}, u32[]{:S(2)}, u32[]{:S(2)}) async-start(bf16[32,16,2560]{2,1,0:T(8,128)(2,1)} %bitcast.24), calls=%async_computation | async-start | bytes 5242880 | tf_op jit(solution)/shard_map/all_to_all | solution.py:375
  84.9 4.6 %collective-permute-start.13 = (bf16[192,768]{1,0:T(8,128)(2,1)}, bf16[192,768]{1,0:T(8,128)(2,1)S(1)}, u32[]{:S(2)}, u32[]{:S(2)}) collective-permute-start(bf16[192,768]{1,0:T(8,128)(2,1)} %copy-done.12), channel_id=1, source_target_pairs={{0,480},{32,0},{64,32},{96,64},{128,96},{160,128},{192,160},{224,1... | collective-permute-start | bytes 884744 | tf_op jit(solution)/shard_map/ppermute | solution.py:402
  94.8 6.7 %collective-permute-done.8.refs_13_ = bf16[192,768]{1,0:T(8,128)(2,1)S(1)} collective-permute-done((bf16[192,768]{1,0:T(8,128)(2,1)}, bf16[192,768]{1,0:T(8,128)(2,1)S(1)}, u32[]{:S(2)}, u32[]{:S(2)}) %collective-permute-start.8) | collective-permute-done | bytes 294944 | tf_op jit(solution)/shard_map/ppermute | solution.py:401
  103.4 4.6 %collective-permute-start.14 = (bf16[192,768]{1,0:T(8,128)(2,1)S(1)}, bf16[192,768]{1,0:T(8,128)(2,1)S(1)}, u32[]{:S(2)}, u32[]{:S(2)}) collective-permute-start(bf16[192,768]{1,0:T(8,128)(2,1)S(1)} %collective-permute-done.13.refs_19_), channel_id=1, source_target_pairs={{0,480},{32,0},{64,32},{96,64},{128,96},{160,128},{192,160},{224,1... | collective-permute-start | bytes 884744 | tf_op jit(solution)/shard_map/ppermute | solution.py:402
  108.0 7.2 %collective-permute-done.18.refs_3_ = bf16[192,768]{1,0:T(8,128)(2,1)S(1)} collective-permute-done((bf16[192,768]{1,0:T(8,128)(2,1)}, bf16[192,768]{1,0:T(8,128)(2,1)S(1)}, u32[]{:S(2)}, u32[]{:S(2)}) %collective-permute-start.18) | collective-permute-done | bytes 294944 | tf_op jit(solution)/shard_map/ppermute | solution.py:404
  115.2 5.3 %collective-permute-start.19 = (bf16[192,768]{1,0:T(8,128)(2,1)S(1)}, bf16[192,768]{1,0:T(8,128)(2,1)S(1)}, u32[]{:S(2)}, u32[]{:S(2)}) collective-permute-start(bf16[192,768]{1,0:T(8,128)(2,1)S(1)} %collective-permute-done.18.refs_3_), channel_id=1, source_target_pairs={{0,480},{32,0},{64,32},{96,64},{128,96},{160,128},{192,160},{224,1... | collective-permute-start | bytes 884744 | tf_op jit(solution)/shard_map/ppermute | solution.py:404
  122.5 4.3 %collective-permute-done.9.refs_12_ = bf16[192,768]{1,0:T(8,128)(2,1)S(1)} collective-permute-done((bf16[192,768]{1,0:T(8,128)(2,1)S(1)}, bf16[192,768]{1,0:T(8,128)(2,1)S(1)}, u32[]{:S(2)}, u32[]{:S(2)}) %collective-permute-start.9) | collective-permute-done | bytes 294944 | tf_op jit(solution)/shard_map/ppermute | solution.py:401
  128.7 4.6 %collective-permute-start.15 = (bf16[192,768]{1,0:T(8,128)(2,1)S(1)}, bf16[192,768]{1,0:T(8,128)(2,1)S(1)}, u32[]{:S(2)}, u32[]{:S(2)}) collective-permute-start(bf16[192,768]{1,0:T(8,128)(2,1)S(1)} %collective-permute-done.14.refs_20_), channel_id=1, source_target_pairs={{0,480},{32,0},{64,32},{96,64},{128,96},{160,128},{192,160},{224,1... | collective-permute-start | bytes 884744 | tf_op jit(solution)/shard_map/ppermute | solution.py:402
  133.3 7.1 %collective-permute-done.19.refs_4_ = bf16[192,768]{1,0:T(8,128)(2,1)S(1)} collective-permute-done((bf16[192,768]{1,0:T(8,128)(2,1)S(1)}, bf16[192,768]{1,0:T(8,128)(2,1)S(1)}, u32[]{:S(2)}, u32[]{:S(2)}) %collective-permute-start.19) | collective-permute-done | bytes 294944 | tf_op jit(solution)/shard_map/ppermute | solution.py:404
  140.4 5.4 %collective-permute-start.20 = (bf16[192,768]{1,0:T(8,128)(2,1)S(1)}, bf16[192,768]{1,0:T(8,128)(2,1)S(1)}, u32[]{:S(2)}, u32[]{:S(2)}) collective-permute-start(bf16[192,768]{1,0:T(8,128)(2,1)S(1)} %collective-permute-done.19.refs_4_), channel_id=1, source_target_pairs={{0,480},{32,0},{64,32},{96,64},{128,96},{160,128},{192,160},{224,1... | collective-permute-start | bytes 884744 | tf_op jit(solution)/shard_map/ppermute | solution.py:404
  147.8 3.9 %collective-permute-done.10.refs_11_ = bf16[192,768]{1,0:T(8,128)(2,1)S(1)} collective-permute-done((bf16[192,768]{1,0:T(8,128)(2,1)S(1)}, bf16[192,768]{1,0:T(8,128)(2,1)S(1)}, u32[]{:S(2)}, u32[]{:S(2)}) %collective-permute-start.10) | collective-permute-done | bytes 294944 | tf_op jit(solution)/shard_map/ppermute | solution.py:401
  153.6 4.8 %collective-permute-start.16 = (bf16[192,768]{1,0:T(8,128)(2,1)S(1)}, bf16[192,768]{1,0:T(8,128)(2,1)S(1)}, u32[]{:S(2)}, u32[]{:S(2)}) collective-permute-start(bf16[192,768]{1,0:T(8,128)(2,1)S(1)} %collective-permute-done.15.refs_21_), channel_id=1, source_target_pairs={{0,480},{32,0},{64,32},{96,64},{128,96},{160,128},{192,160},{224,1... | collective-permute-start | bytes 884744 | tf_op jit(solution)/shard_map/ppermute | solution.py:402
  158.5 7.2 %collective-permute-done.20.refs_5_ = bf16[192,768]{1,0:T(8,128)(2,1)S(1)} collective-permute-done((bf16[192,768]{1,0:T(8,128)(2,1)S(1)}, bf16[192,768]{1,0:T(8,128)(2,1)S(1)}, u32[]{:S(2)}, u32[]{:S(2)}) %collective-permute-start.20) | collective-permute-done | bytes 294944 | tf_op jit(solution)/shard_map/ppermute | solution.py:404
  165.7 5.4 %collective-permute-start.21 = (bf16[192,768]{1,0:T(8,128)(2,1)S(1)}, bf16[192,768]{1,0:T(8,128)(2,1)}, u32[]{:S(2)}, u32[]{:S(2)}) collective-permute-start(bf16[192,768]{1,0:T(8,128)(2,1)S(1)} %collective-permute-done.20.refs_5_), channel_id=1, source_target_pairs={{0,480},{32,0},{64,32},{96,64},{128,96},{160,128},{192,160},{224,1... | collective-permute-start | bytes 884744 | tf_op jit(solution)/shard_map/ppermute | solution.py:404
  173.1 3.9 %collective-permute-done.11.refs_10_ = bf16[192,768]{1,0:T(8,128)(2,1)S(1)} collective-permute-done((bf16[192,768]{1,0:T(8,128)(2,1)S(1)}, bf16[192,768]{1,0:T(8,128)(2,1)S(1)}, u32[]{:S(2)}, u32[]{:S(2)}) %collective-permute-start.11) | collective-permute-done | bytes 294944 | tf_op jit(solution)/shard_map/ppermute | solution.py:401
  178.9 4.8 %collective-permute-start.17 = (bf16[192,768]{1,0:T(8,128)(2,1)S(1)}, bf16[192,768]{1,0:T(8,128)(2,1)}, u32[]{:S(2)}, u32[]{:S(2)}) collective-permute-start(bf16[192,768]{1,0:T(8,128)(2,1)S(1)} %collective-permute-done.16.refs_22_), channel_id=1, source_target_pairs={{0,480},{32,0},{64,32},{96,64},{128,96},{160,128},{192,160},{224,1... | collective-permute-start | bytes 884744 | tf_op jit(solution)/shard_map/ppermute | solution.py:402
  183.7 7.2 %collective-permute-done.21.refs_6_ = bf16[192,768]{1,0:T(8,128)(2,1)} collective-permute-done((bf16[192,768]{1,0:T(8,128)(2,1)S(1)}, bf16[192,768]{1,0:T(8,128)(2,1)}, u32[]{:S(2)}, u32[]{:S(2)}) %collective-permute-start.21) | collective-permute-done | bytes 294944 | tf_op jit(solution)/shard_map/ppermute | solution.py:404
  190.9 5.4 %collective-permute-start.22 = (bf16[192,768]{1,0:T(8,128)(2,1)}, bf16[192,768]{1,0:T(8,128)(2,1)}, u32[]{:S(2)}, u32[]{:S(2)}) collective-permute-start(bf16[192,768]{1,0:T(8,128)(2,1)} %collective-permute-done.21.refs_6_), channel_id=1, source_target_pairs={{0,480},{32,0},{64,32},{96,64},{128,96},{160,128},{192,160},{224,1... | collective-permute-start | bytes 884744 | tf_op jit(solution)/shard_map/ppermute | solution.py:404
  198.3 4.0 %collective-permute-done.12.refs_9_ = bf16[192,768]{1,0:T(8,128)(2,1)} collective-permute-done((bf16[192,768]{1,0:T(8,128)(2,1)S(1)}, bf16[192,768]{1,0:T(8,128)(2,1)}, u32[]{:S(2)}, u32[]{:S(2)}) %collective-permute-start.12) | collective-permute-done | bytes 294944 | tf_op jit(solution)/shard_map/ppermute | solution.py:401
  204.2 4.6 %collective-permute-start.24 = (bf16[192,768]{1,0:T(8,128)(2,1)}, bf16[192,768]{1,0:T(8,128)(2,1)}, u32[]{:S(2)}, u32[]{:S(2)}) collective-permute-start(bf16[192,768]{1,0:T(8,128)(2,1)} %collective-permute-done.17.refs_23_), channel_id=1, source_target_pairs={{0,480},{32,0},{64,32},{96,64},{128,96},{160,128},{192,160},{224,1... | collective-permute-start | bytes 884744 | tf_op jit(solution)/shard_map/ppermute | solution.py:402
  214.5 10.4 %shard_map.104 = bf16[256,2560]{1,0:T(8,128)(2,1)} custom-call(s32[1]{0:T(128)} %bitcast.16.me, bf16[2,320,2048]{2,1,0:T(8,128)(2,1)} %copy-done, bf16[192,768]{1,0:T(8,128)(2,1)} %get-tuple-element.15.refs_0_, bf16[192,768]{1,0:T(8,128)(2,1)} %copy-done.9, bf16[192,768]{1,0:T(8,128)(2,1)} %copy-done.13, bf16[192,768]{1,0:T(8,128)(2,1)} %copy-done.17, ...), custom_call_target="tpu_custom_call" | custom-call | flops 3019898880 | bytes 13631488 | tf_op jit(solution)/shard_map/pallas_call | solution.py:339
  224.9 8.8 %all-to-all-start.2 = ((bf16[32,8,2560]{2,1,0:T(8,128)(2,1)}), bf16[32,8,2560]{2,1,0:T(8,128)(2,1)S(1)}, u32[]{:S(2)}, u32[]{:S(2)}) async-start(bf16[32,8,2560]{2,1,0:T(8,128)(2,1)} %bitcast.32), calls=%async_computation.2 | async-start | bytes 2621440 | tf_op jit(solution)/shard_map/all_to_all | solution.py:375
  233.7 8.0 %shard_map.103 = bf16[256,2560]{1,0:T(8,128)(2,1)} custom-call(bf16[2,320,2048]{2,1,0:T(8,128)(2,1)} %copy-done, bf16[16,384,768]{2,1,0:T(8,128)(2,1)} %bitcast.30), custom_call_target="tpu_custom_call" | custom-call | flops 3019898880 | bytes 13631488 | tf_op jit(solution)/shard_map/pallas_call | solution.py:322
  241.7 11.7 %all-to-all-done.2 = bf16[32,8,2560]{2,1,0:T(8,128)(2,1)S(1)} async-done(((bf16[32,8,2560]{2,1,0:T(8,128)(2,1)}), bf16[32,8,2560]{2,1,0:T(8,128)(2,1)S(1)}, u32[]{:S(2)}, u32[]{:S(2)}) %all-to-all-start.2) | async-done | bytes 1310752 | tf_op jit(solution)/shard_map/all_to_all | solution.py:375
  253.5 4.0 %all-to-all-start.1 = ((bf16[32,8,2560]{2,1,0:T(8,128)(2,1)}), bf16[32,8,2560]{2,1,0:T(8,128)(2,1)S(1)}, u32[]{:S(2)}, u32[]{:S(2)}) async-start(bf16[32,8,2560]{2,1,0:T(8,128)(2,1)} %bitcast.31), calls=%async_computation.1 | async-start | bytes 2621440 | tf_op jit(solution)/shard_map/all_to_all | solution.py:375
  259.2 18.2 %all-to-all-done.1 = bf16[32,8,2560]{2,1,0:T(8,128)(2,1)S(1)} async-done(((bf16[32,8,2560]{2,1,0:T(8,128)(2,1)}), bf16[32,8,2560]{2,1,0:T(8,128)(2,1)S(1)}, u32[]{:S(2)}, u32[]{:S(2)}) %all-to-all-start.1) | async-done | bytes 1310752 | tf_op jit(solution)/shard_map/all_to_all | solution.py:375
  (111 shorter events, 58.2 us)
Async XLA Ops:
  6.5 227.2 %all-gather.3.cloned.1.call-start = ((), (), s32[]{:S(2)}) async-start(), calls=%async_computation.3 | async-start | bytes 10027008 | tf_op jit(solution)/shard_map/all_gather | solution.py:396
  8.9 19.2 %collective-permute-start = (bf16[192,768]{1,0:T(8,128)(2,1)}, bf16[192,768]{1,0:T(8,128)(2,1)S(1)}, u32[]{:S(2)}, u32[]{:S(2)}) collective-permute-start(bf16[192,768]{1,0:T(8,128)(2,1)} %get-tuple-element.15.refs_0_), channel_id=1, source_target_pairs={{0,32},{32,64},{64,96},{96,128},{128,160},{160,192},{192,224},{224... | collective-permute-start | bytes 884744 | tf_op jit(solution)/shard_map/ppermute | solution.py:401
  13.3 16.8 %collective-permute-start.2 = (bf16[192,768]{1,0:T(8,128)(2,1)}, bf16[192,768]{1,0:T(8,128)(2,1)S(1)}, u32[]{:S(2)}, u32[]{:S(2)}) collective-permute-start(bf16[192,768]{1,0:T(8,128)(2,1)} %get-tuple-element.16.refs_16_), channel_id=1, source_target_pairs={{0,480},{32,0},{64,32},{96,64},{128,96},{160,128},{192,160},{224,1... | collective-permute-start | bytes 884744 | tf_op jit(solution)/shard_map/ppermute | solution.py:402
  22.8 15.6 %collective-permute-start.4 = (bf16[192,768]{1,0:T(8,128)(2,1)}, bf16[192,768]{1,0:T(8,128)(2,1)S(1)}, u32[]{:S(2)}, u32[]{:S(2)}) collective-permute-start(bf16[192,768]{1,0:T(8,128)(2,1)} %get-tuple-element.15.refs_0_), channel_id=1, source_target_pairs={{0,480},{32,0},{64,32},{96,64},{128,96},{160,128},{192,160},{224,1... | collective-permute-start | bytes 884744 | tf_op jit(solution)/shard_map/ppermute | solution.py:404
  26.1 17.5 %collective-permute-start.6 = (bf16[192,768]{1,0:T(8,128)(2,1)}, bf16[192,768]{1,0:T(8,128)(2,1)S(1)}, u32[]{:S(2)}, u32[]{:S(2)}) collective-permute-start(bf16[192,768]{1,0:T(8,128)(2,1)} %get-tuple-element.16.refs_16_), channel_id=1, source_target_pairs={{0,32},{32,64},{64,96},{96,128},{128,160},{160,192},{192,224},{224... | collective-permute-start | bytes 884744 | tf_op jit(solution)/shard_map/ppermute | solution.py:405
  28.1 22.7 %collective-permute-start.1 = (bf16[192,768]{1,0:T(8,128)(2,1)S(1)}, bf16[192,768]{1,0:T(8,128)(2,1)S(1)}, u32[]{:S(2)}, u32[]{:S(2)}) collective-permute-start(bf16[192,768]{1,0:T(8,128)(2,1)S(1)} %collective-permute-done.refs_15_), channel_id=1, source_target_pairs={{0,32},{32,64},{64,96},{96,128},{128,160},{160,192},{192,224},{224... | collective-permute-start | bytes 884744 | tf_op jit(solution)/shard_map/ppermute | solution.py:401
  30.0 20.9 %collective-permute-start.3 = (bf16[192,768]{1,0:T(8,128)(2,1)S(1)}, bf16[192,768]{1,0:T(8,128)(2,1)S(1)}, u32[]{:S(2)}, u32[]{:S(2)}) collective-permute-start(bf16[192,768]{1,0:T(8,128)(2,1)S(1)} %collective-permute-done.2.refs_17_), channel_id=1, source_target_pairs={{0,480},{32,0},{64,32},{96,64},{128,96},{160,128},{192,160},{224,1... | collective-permute-start | bytes 884744 | tf_op jit(solution)/shard_map/ppermute | solution.py:402
  38.4 25.2 %collective-permute-start.5 = (bf16[192,768]{1,0:T(8,128)(2,1)S(1)}, bf16[192,768]{1,0:T(8,128)(2,1)S(1)}, u32[]{:S(2)}, u32[]{:S(2)}) collective-permute-start(bf16[192,768]{1,0:T(8,128)(2,1)S(1)} %collective-permute-done.4.refs_1_), channel_id=1, source_target_pairs={{0,480},{32,0},{64,32},{96,64},{128,96},{160,128},{192,160},{224,1... | collective-permute-start | bytes 884744 | tf_op jit(solution)/shard_map/ppermute | solution.py:404
  43.7 19.8 %collective-permute-start.7 = (bf16[192,768]{1,0:T(8,128)(2,1)S(1)}, bf16[192,768]{1,0:T(8,128)(2,1)S(1)}, u32[]{:S(2)}, u32[]{:S(2)}) collective-permute-start(bf16[192,768]{1,0:T(8,128)(2,1)S(1)} %collective-permute-done.6.refs_31_), channel_id=1, source_target_pairs={{0,32},{32,64},{64,96},{96,128},{128,160},{160,192},{192,224},{224... | collective-permute-start | bytes 884744 | tf_op jit(solution)/shard_map/ppermute | solution.py:405
  70.4 138.4 %all-to-all-start = ((bf16[32,16,2560]{2,1,0:T(8,128)(2,1)}), bf16[32,16,2560]{2,1,0:T(8,128)(2,1)S(1)}, u32[]{:S(2)}, u32[]{:S(2)}) async-start(bf16[32,16,2560]{2,1,0:T(8,128)(2,1)} %bitcast.24), calls=%async_computation | async-start | bytes 5242880 | tf_op jit(solution)/shard_map/all_to_all | solution.py:375
  83.0 18.5 %collective-permute-start.8 = (bf16[192,768]{1,0:T(8,128)(2,1)}, bf16[192,768]{1,0:T(8,128)(2,1)S(1)}, u32[]{:S(2)}, u32[]{:S(2)}) collective-permute-start(bf16[192,768]{1,0:T(8,128)(2,1)} %copy-done.11), channel_id=1, source_target_pairs={{0,32},{32,64},{64,96},{96,128},{128,160},{160,192},{192,224},{224... | collective-permute-start | bytes 884744 | tf_op jit(solution)/shard_map/ppermute | solution.py:401
  84.9 18.5 %collective-permute-start.13 = (bf16[192,768]{1,0:T(8,128)(2,1)}, bf16[192,768]{1,0:T(8,128)(2,1)S(1)}, u32[]{:S(2)}, u32[]{:S(2)}) collective-permute-start(bf16[192,768]{1,0:T(8,128)(2,1)} %copy-done.12), channel_id=1, source_target_pairs={{0,480},{32,0},{64,32},{96,64},{128,96},{160,128},{192,160},{224,1... | collective-permute-start | bytes 884744 | tf_op jit(solution)/shard_map/ppermute | solution.py:402
  89.5 25.7 %collective-permute-start.18 = (bf16[192,768]{1,0:T(8,128)(2,1)}, bf16[192,768]{1,0:T(8,128)(2,1)S(1)}, u32[]{:S(2)}, u32[]{:S(2)}) collective-permute-start(bf16[192,768]{1,0:T(8,128)(2,1)} %copy-done.13), channel_id=1, source_target_pairs={{0,480},{32,0},{64,32},{96,64},{128,96},{160,128},{192,160},{224,1... | collective-permute-start | bytes 884744 | tf_op jit(solution)/shard_map/ppermute | solution.py:404
  92.5 28.1 %collective-permute-start.25 = (bf16[192,768]{1,0:T(8,128)(2,1)}, bf16[192,768]{1,0:T(8,128)(2,1)S(1)}, u32[]{:S(2)}, u32[]{:S(2)}) collective-permute-start(bf16[192,768]{1,0:T(8,128)(2,1)} %copy-done.14), channel_id=1, source_target_pairs={{0,32},{32,64},{64,96},{96,128},{128,160},{160,192},{192,224},{224... | collective-permute-start | bytes 884744 | tf_op jit(solution)/shard_map/ppermute | solution.py:405
  101.5 25.3 %collective-permute-start.9 = (bf16[192,768]{1,0:T(8,128)(2,1)S(1)}, bf16[192,768]{1,0:T(8,128)(2,1)S(1)}, u32[]{:S(2)}, u32[]{:S(2)}) collective-permute-start(bf16[192,768]{1,0:T(8,128)(2,1)S(1)} %collective-permute-done.8.refs_13_), channel_id=1, source_target_pairs={{0,32},{32,64},{64,96},{96,128},{128,160},{160,192},{192,224},{224... | collective-permute-start | bytes 884744 | tf_op jit(solution)/shard_map/ppermute | solution.py:401
  103.4 25.3 %collective-permute-start.14 = (bf16[192,768]{1,0:T(8,128)(2,1)S(1)}, bf16[192,768]{1,0:T(8,128)(2,1)S(1)}, u32[]{:S(2)}, u32[]{:S(2)}) collective-permute-start(bf16[192,768]{1,0:T(8,128)(2,1)S(1)} %collective-permute-done.13.refs_19_), channel_id=1, source_target_pairs={{0,480},{32,0},{64,32},{96,64},{128,96},{160,128},{192,160},{224,1... | collective-permute-start | bytes 884744 | tf_op jit(solution)/shard_map/ppermute | solution.py:402
  115.2 25.2 %collective-permute-start.19 = (bf16[192,768]{1,0:T(8,128)(2,1)S(1)}, bf16[192,768]{1,0:T(8,128)(2,1)S(1)}, u32[]{:S(2)}, u32[]{:S(2)}) collective-permute-start(bf16[192,768]{1,0:T(8,128)(2,1)S(1)} %collective-permute-done.18.refs_3_), channel_id=1, source_target_pairs={{0,480},{32,0},{64,32},{96,64},{128,96},{160,128},{192,160},{224,1... | collective-permute-start | bytes 884744 | tf_op jit(solution)/shard_map/ppermute | solution.py:404
  120.5 25.3 %collective-permute-start.26 = (bf16[192,768]{1,0:T(8,128)(2,1)S(1)}, bf16[192,768]{1,0:T(8,128)(2,1)S(1)}, u32[]{:S(2)}, u32[]{:S(2)}) collective-permute-start(bf16[192,768]{1,0:T(8,128)(2,1)S(1)} %collective-permute-done.25.refs_29_), channel_id=1, source_target_pairs={{0,32},{32,64},{64,96},{96,128},{128,160},{160,192},{192,224},{224... | collective-permute-start | bytes 884744 | tf_op jit(solution)/shard_map/ppermute | solution.py:405
  126.8 24.9 %collective-permute-start.10 = (bf16[192,768]{1,0:T(8,128)(2,1)S(1)}, bf16[192,768]{1,0:T(8,128)(2,1)S(1)}, u32[]{:S(2)}, u32[]{:S(2)}) collective-permute-start(bf16[192,768]{1,0:T(8,128)(2,1)S(1)} %collective-permute-done.9.refs_12_), channel_id=1, source_target_pairs={{0,32},{32,64},{64,96},{96,128},{128,160},{160,192},{192,224},{224... | collective-permute-start | bytes 884744 | tf_op jit(solution)/shard_map/ppermute | solution.py:401
  128.7 24.9 %collective-permute-start.15 = (bf16[192,768]{1,0:T(8,128)(2,1)S(1)}, bf16[192,768]{1,0:T(8,128)(2,1)S(1)}, u32[]{:S(2)}, u32[]{:S(2)}) collective-permute-start(bf16[192,768]{1,0:T(8,128)(2,1)S(1)} %collective-permute-done.14.refs_20_), channel_id=1, source_target_pairs={{0,480},{32,0},{64,32},{96,64},{128,96},{160,128},{192,160},{224,1... | collective-permute-start | bytes 884744 | tf_op jit(solution)/shard_map/ppermute | solution.py:402
  140.4 25.3 %collective-permute-start.20 = (bf16[192,768]{1,0:T(8,128)(2,1)S(1)}, bf16[192,768]{1,0:T(8,128)(2,1)S(1)}, u32[]{:S(2)}, u32[]{:S(2)}) collective-permute-start(bf16[192,768]{1,0:T(8,128)(2,1)S(1)} %collective-permute-done.19.refs_4_), channel_id=1, source_target_pairs={{0,480},{32,0},{64,32},{96,64},{128,96},{160,128},{192,160},{224,1... | collective-permute-start | bytes 884744 | tf_op jit(solution)/shard_map/ppermute | solution.py:404
  145.8 25.3 %collective-permute-start.27 = (bf16[192,768]{1,0:T(8,128)(2,1)S(1)}, bf16[192,768]{1,0:T(8,128)(2,1)S(1)}, u32[]{:S(2)}, u32[]{:S(2)}) collective-permute-start(bf16[192,768]{1,0:T(8,128)(2,1)S(1)} %collective-permute-done.26.refs_28_), channel_id=1, source_target_pairs={{0,32},{32,64},{64,96},{96,128},{128,160},{160,192},{192,224},{224... | collective-permute-start | bytes 884744 | tf_op jit(solution)/shard_map/ppermute | solution.py:405
  151.7 25.3 %collective-permute-start.11 = (bf16[192,768]{1,0:T(8,128)(2,1)S(1)}, bf16[192,768]{1,0:T(8,128)(2,1)S(1)}, u32[]{:S(2)}, u32[]{:S(2)}) collective-permute-start(bf16[192,768]{1,0:T(8,128)(2,1)S(1)} %collective-permute-done.10.refs_11_), channel_id=1, source_target_pairs={{0,32},{32,64},{64,96},{96,128},{128,160},{160,192},{192,224},{224... | collective-permute-start | bytes 884744 | tf_op jit(solution)/shard_map/ppermute | solution.py:401
  153.6 25.3 %collective-permute-start.16 = (bf16[192,768]{1,0:T(8,128)(2,1)S(1)}, bf16[192,768]{1,0:T(8,128)(2,1)S(1)}, u32[]{:S(2)}, u32[]{:S(2)}) collective-permute-start(bf16[192,768]{1,0:T(8,128)(2,1)S(1)} %collective-permute-done.15.refs_21_), channel_id=1, source_target_pairs={{0,480},{32,0},{64,32},{96,64},{128,96},{160,128},{192,160},{224,1... | collective-permute-start | bytes 884744 | tf_op jit(solution)/shard_map/ppermute | solution.py:402
  165.7 25.3 %collective-permute-start.21 = (bf16[192,768]{1,0:T(8,128)(2,1)S(1)}, bf16[192,768]{1,0:T(8,128)(2,1)}, u32[]{:S(2)}, u32[]{:S(2)}) collective-permute-start(bf16[192,768]{1,0:T(8,128)(2,1)S(1)} %collective-permute-done.20.refs_5_), channel_id=1, source_target_pairs={{0,480},{32,0},{64,32},{96,64},{128,96},{160,128},{192,160},{224,1... | collective-permute-start | bytes 884744 | tf_op jit(solution)/shard_map/ppermute | solution.py:404
  171.1 25.2 %collective-permute-start.28 = (bf16[192,768]{1,0:T(8,128)(2,1)S(1)}, bf16[192,768]{1,0:T(8,128)(2,1)}, u32[]{:S(2)}, u32[]{:S(2)}) collective-permute-start(bf16[192,768]{1,0:T(8,128)(2,1)S(1)} %collective-permute-done.27.refs_27_), channel_id=1, source_target_pairs={{0,32},{32,64},{64,96},{96,128},{128,160},{160,192},{192,224},{224... | collective-permute-start | bytes 884744 | tf_op jit(solution)/shard_map/ppermute | solution.py:405
  177.0 25.3 %collective-permute-start.12 = (bf16[192,768]{1,0:T(8,128)(2,1)S(1)}, bf16[192,768]{1,0:T(8,128)(2,1)}, u32[]{:S(2)}, u32[]{:S(2)}) collective-permute-start(bf16[192,768]{1,0:T(8,128)(2,1)S(1)} %collective-permute-done.11.refs_10_), channel_id=1, source_target_pairs={{0,32},{32,64},{64,96},{96,128},{128,160},{160,192},{192,224},{224... | collective-permute-start | bytes 884744 | tf_op jit(solution)/shard_map/ppermute | solution.py:401
  178.9 25.3 %collective-permute-start.17 = (bf16[192,768]{1,0:T(8,128)(2,1)S(1)}, bf16[192,768]{1,0:T(8,128)(2,1)}, u32[]{:S(2)}, u32[]{:S(2)}) collective-permute-start(bf16[192,768]{1,0:T(8,128)(2,1)S(1)} %collective-permute-done.16.refs_22_), channel_id=1, source_target_pairs={{0,480},{32,0},{64,32},{96,64},{128,96},{160,128},{192,160},{224,1... | collective-permute-start | bytes 884744 | tf_op jit(solution)/shard_map/ppermute | solution.py:402
  190.9 21.4 %collective-permute-start.22 = (bf16[192,768]{1,0:T(8,128)(2,1)}, bf16[192,768]{1,0:T(8,128)(2,1)}, u32[]{:S(2)}, u32[]{:S(2)}) collective-permute-start(bf16[192,768]{1,0:T(8,128)(2,1)} %collective-permute-done.21.refs_6_), channel_id=1, source_target_pairs={{0,480},{32,0},{64,32},{96,64},{128,96},{160,128},{192,160},{224,1... | collective-permute-start | bytes 884744 | tf_op jit(solution)/shard_map/ppermute | solution.py:404
  196.4 16.0 %collective-permute-start.29 = (bf16[192,768]{1,0:T(8,128)(2,1)}, bf16[192,768]{1,0:T(8,128)(2,1)}, u32[]{:S(2)}, u32[]{:S(2)}) collective-permute-start(bf16[192,768]{1,0:T(8,128)(2,1)} %collective-permute-done.28.refs_26_), channel_id=1, source_target_pairs={{0,32},{32,64},{64,96},{96,128},{128,160},{160,192},{192,224},{224... | collective-permute-start | bytes 884744 | tf_op jit(solution)/shard_map/ppermute | solution.py:405
  224.9 28.6 %all-to-all-start.2 = ((bf16[32,8,2560]{2,1,0:T(8,128)(2,1)}), bf16[32,8,2560]{2,1,0:T(8,128)(2,1)S(1)}, u32[]{:S(2)}, u32[]{:S(2)}) async-start(bf16[32,8,2560]{2,1,0:T(8,128)(2,1)} %bitcast.32), calls=%async_computation.2 | async-start | bytes 2621440 | tf_op jit(solution)/shard_map/all_to_all | solution.py:375
  253.5 23.9 %all-to-all-start.1 = ((bf16[32,8,2560]{2,1,0:T(8,128)(2,1)}), bf16[32,8,2560]{2,1,0:T(8,128)(2,1)S(1)}, u32[]{:S(2)}, u32[]{:S(2)}) async-start(bf16[32,8,2560]{2,1,0:T(8,128)(2,1)} %bitcast.31), calls=%async_computation.1 | async-start | bytes 2621440 | tf_op jit(solution)/shard_map/all_to_all | solution.py:375
  (31 other events, 563.5 us)
Sparse Core Ops, SparseCore 0:
  9.4 193.6 all-gather.2
